TPU v7x, 512 devices: a whole 4x4x16 slice. The times are simulated.
512 devices in a mesh: dp: 32 (over z, core), ctx: 16 (over y, x).
Axes of the slice: x: 4, y: 4, z: 16, core: 2. Of those that a mesh axis runs over, the one named last changes fastest.
Arguments:
- queries: bfloat16 [4, 64, 128, 576], P(None, 'dp', 'ctx'), may hold values from -14 to 14
- latent_cache: bfloat16 [64, 24576, 576], P('dp', 'ctx'), may hold values from -7 to 7
- new_latent: bfloat16 [4, 64, 576], P(None, 'dp'), may hold values from -12 to 12
- lengths: int32 [64], P('dp'), may hold values from 3072 to 24576, as said below
- value_up: bfloat16 [128, 512, 128], P('ctx', 'dp'), may hold values from -0.25 to 0.25
Outputs:
- attended: float32 [4, 64, 128, 128], P(None, 'dp', 'ctx')
Inputs may be any that keep to these rules, and one draw needn't show every extreme that they name: Row b's cache holds live entries at positions 0 to lengths[b] - 1 and some row's length is 24576 in every draw.
All inputs are finite; a program needn't handle non-finite values.
Results may differ from a plain program's by a relative error of at most 0.006.
Values may be sent and summed in bfloat16 or wider, within the bound.
No kernel may reach another device: no remote copies, remote signals or barrier semaphores. Data moves between devices by JAX's collectives and lax.ppermute only.
A program may use at most 64 MiB of HBM per device.

v0:
```python
import jax
import jax.numpy as jnp
from jax import lax
from jax.sharding import PartitionSpec as P

LAT = 512
ROPE = 64
NOPE = 128


def rotate(values, positions):
    half_width = values.shape[-1] // 2
    pair_index = jnp.arange(half_width, dtype=jnp.float32)
    frequency = jnp.power(jnp.float32(10000.0), -2.0 * pair_index / values.shape[-1])
    angles = positions.astype(jnp.float32)[..., None] * frequency
    first_half = values[..., :half_width].astype(jnp.float32)
    second_half = values[..., half_width:].astype(jnp.float32)
    cosine = jnp.cos(angles)
    sine_part = jnp.sin(angles)
    return jnp.concatenate(
        [
            first_half * cosine - second_half * sine_part,
            first_half * sine_part + second_half * cosine,
        ],
        axis=-1,
    )


def shard_partial(present, key_rows, valid_mask, score_scale):
    scores = (
        jnp.einsum("bhc,bkc->bhk", present, key_rows, preferred_element_type=jnp.float32)
        * score_scale
    )
    row_top = jnp.max(jnp.where(valid_mask, scores, -1e30), axis=-1)
    weights = jnp.where(valid_mask, jnp.exp(scores - row_top[..., None]), 0.0)
    weight_sum = jnp.sum(weights, axis=-1)
    mixed = jnp.einsum(
        "bhk,bkl->bhl",
        weights.astype(jnp.bfloat16),
        key_rows[..., :LAT],
        preferred_element_type=jnp.float32,
    )
    filled = weight_sum > 0
    safe_sum = jnp.where(filled, weight_sum, 1.0)
    return (mixed / safe_sum[..., None], jnp.where(filled, row_top + jnp.log(safe_sum), -1e30))


def merge_exchanged(pieces, spreads, fresh, fresh_lse):
    peak_all = jnp.maximum(jnp.max(spreads, axis=0), fresh_lse)
    factors = jnp.exp(spreads - peak_all[None])
    extra_weight = jnp.exp(fresh_lse - peak_all)
    total = jnp.sum(factors[..., None] * pieces, axis=0) + extra_weight[..., None] * fresh
    return total / (jnp.sum(factors, axis=0) + extra_weight)[..., None]


def body(queries, latent_cache, new_latent, lengths, value_up):
    step_count = queries.shape[0]
    shard_span = latent_cache.shape[1]
    score_scale = (NOPE + ROPE) ** (-0.5)
    step_ids = jnp.arange(step_count, dtype=jnp.int32)
    positions = lengths[None, :] + step_ids[:, None]
    query_ready = jnp.concatenate(
        [
            queries[..., :LAT],
            rotate(queries[..., LAT:], positions[:, :, None]).astype(jnp.bfloat16),
        ],
        axis=-1,
    )
    new_ready = jnp.concatenate(
        [new_latent[..., :LAT], rotate(new_latent[..., LAT:], positions).astype(jnp.bfloat16)],
        axis=-1,
    )
    new_keys = jnp.swapaxes(new_ready, 0, 1)
    slot_ids = lax.axis_index("ctx") * shard_span + jnp.arange(shard_span, dtype=jnp.int32)
    cache_valid = (slot_ids[None, :] < lengths[:, None])[:, None, :]
    latents = []
    for current in range(step_count):
        present = lax.all_gather(query_ready[current], "ctx", axis=1, tiled=True)
        parted, spread = shard_partial(present, latent_cache, cache_valid, score_scale)
        new_valid = (step_ids <= current)[None, None, :]
        fresh, fresh_lse = shard_partial(query_ready[current], new_keys, new_valid, score_scale)
        pieces, spreads = (
            lax.all_to_all(parted[None], "ctx", split_axis=2, concat_axis=0, tiled=True),
            lax.all_to_all(spread[None], "ctx", split_axis=2, concat_axis=0, tiled=True),
        )
        merged = merge_exchanged(pieces, spreads, fresh, fresh_lse)
        latents.append(merged.astype(jnp.bfloat16))
    stacked = jnp.stack(latents, axis=0)
    return jnp.einsum(
        "sbhl,hlv->sbhv",
        stacked,
        lax.all_gather(value_up, "dp", axis=1, tiled=True),
        preferred_element_type=jnp.float32,
    )


def solution(mesh):
    placed = (
        P(None, "dp", "ctx", None),
        P("dp", "ctx", None),
        P(None, "dp", None),
        P("dp"),
        P("ctx", "dp", None),
    )
    return jax.shard_map(
        body, mesh=mesh, in_specs=placed, out_specs=P(None, "dp", "ctx", None), check_vma=False
    )
```

profile of v0, /device:TPU:256, one launch (start us, length us, event | category | flops | bytes accessed | tf_op | source)
XLA Modules:
  0.0 271.1 jit_solution(5752275151726588549)
XLA Ops:
  12.1 26.1 %all-gather = bf16[1,2,128,576]{3,1,0,2:T(2,128)(2,1)} all-gather(bf16[1,2,8,576]{3,1,0,2:T(2,128)(2,1)S(1)} %copy.84), channel_id=2, replica_groups=mesh['dp'=32,'ctx'=16] {'ctx'}, dimensions={2}, use_global_device_ids=true | all-gather | bytes 313344 | tf_op jit(solution)/shard_map/all_gather | solution.py:78
  40.9 25.1 %all-gather.3 = bf16[1,2,128,576]{3,1,0,2:T(2,128)(2,1)} all-gather(bf16[1,2,8,576]{3,1,0,2:T(2,128)(2,1)S(1)} %copy.109), channel_id=5, replica_groups=mesh['dp'=32,'ctx'=16] {'ctx'}, dimensions={2}, use_global_device_ids=true | all-gather | bytes 313344 | tf_op jit(solution)/shard_map/all_gather | solution.py:78
  68.7 23.5 %all-gather.2 = bf16[1,2,128,576]{3,1,0,2:T(2,128)(2,1)} all-gather(bf16[1,2,8,576]{3,1,0,2:T(2,128)(2,1)S(1)} %copy.102), channel_id=4, replica_groups=mesh['dp'=32,'ctx'=16] {'ctx'}, dimensions={2}, use_global_device_ids=true | all-gather | bytes 313344 | tf_op jit(solution)/shard_map/all_gather | solution.py:78
  94.1 3.0 %convolution_multiply_fusion = f32[2,128,1536]{2,1,0:T(8,128)} fusion(bf16[2,1536,576]{1,2,0:T(8,128)(2,1)S(1)} %copy-done, bf16[1,2,128,576]{2,3,1,0:T(8,128)(2,1)} %copy.110), kind=kOutput, calls=%fused_computation | convolution fusion | flops 453378048 | bytes 5406720 | tf_op jit(solution)/shard_map/bhc,bkc->bhk/dot_general | solution.py:31
  99.1 25.1 %all-gather.1 = bf16[1,2,128,576]{3,1,0,2:T(2,128)(2,1)} all-gather(bf16[1,2,8,576]{3,1,0,2:T(2,128)(2,1)S(1)} %copy.95), channel_id=3, replica_groups=mesh['dp'=32,'ctx'=16] {'ctx'}, dimensions={2}, use_global_device_ids=true | all-gather | bytes 313344 | tf_op jit(solution)/shard_map/all_gather | solution.py:78
  126.2 2.0 select_reduce_fusion.3
  134.4 4.2 %all-to-all-start.2 = ((f32[1,2,128]{1,0,2:T(1,128)}), f32[1,2,128]{1,0,2:T(1,128)}, u32[]{:S(2)}, u32[]{:S(2)}) async-start(f32[1,2,128]{1,0,2:T(1,128)} %copy.97), calls=%async_computation.2 | async-start | bytes 131072 | tf_op jit(solution)/shard_map/all_to_all | solution.py:84
  147.7 3.5 %fusion.45 = f32[1,2,128,512]{3,2,1,0:T(8,128)} fusion(bf16[2,1536,576]{1,2,0:T(8,128)(2,1)S(1)} %copy-done, f32[2,128,1536]{2,1,0:T(8,128)} %copy-done.5, f32[2,128]{1,0:T(2,128)} %copy-done.15, pred[2,1536]{1,0:T(4,128)(4,1)S(1)} %broadcast_compare_fusion, f32[2,128]{1,0:T(2,128)S(1)} %compare_select_fusion.3), kind=kOutput, calls=%fused_computation.60 | convolution fusion | flops 403963904 | bytes 5251072 | tf_op jit(solution)/shard_map/bhk,bkl->bhl/dot_general | solution.py:37
  159.4 2.3 copy.93
  161.6 2.2 copy.100
  167.8 7.2 %all-to-all-start = ((f32[1,2,128]{1,0,2:T(1,128)}), f32[1,2,128]{1,0,2:T(1,128)S(1)}, u32[]{:S(2)}, u32[]{:S(2)}) async-start(f32[1,2,128]{1,0,2:T(1,128)} %copy.86), calls=%async_computation | async-start | bytes 131072 | tf_op jit(solution)/shard_map/all_to_all | solution.py:84
  175.9 6.6 %all-to-all-done = f32[1,2,128]{1,0,2:T(1,128)S(1)} async-done(((f32[1,2,128]{1,0,2:T(1,128)}), f32[1,2,128]{1,0,2:T(1,128)S(1)}, u32[]{:S(2)}, u32[]{:S(2)}) %all-to-all-start) | async-done | bytes 1056 | tf_op jit(solution)/shard_map/all_to_all | solution.py:84
  182.6 3.5 %all-to-all-start.6 = ((f32[1,2,128]{1,0,2:T(1,128)}), f32[1,2,128]{1,0,2:T(1,128)S(1)}, u32[]{:S(2)}, u32[]{:S(2)}) async-start(f32[1,2,128]{1,0,2:T(1,128)} %copy.111), calls=%async_computation.6 | async-start | bytes 131072 | tf_op jit(solution)/shard_map/all_to_all | solution.py:84
  186.3 7.4 %all-to-all-done.6 = f32[1,2,128]{1,0,2:T(1,128)S(1)} async-done(((f32[1,2,128]{1,0,2:T(1,128)}), f32[1,2,128]{1,0,2:T(1,128)S(1)}, u32[]{:S(2)}, u32[]{:S(2)}) %all-to-all-start.6) | async-done | bytes 1056 | tf_op jit(solution)/shard_map/all_to_all | solution.py:84
  193.7 3.5 %all-to-all-start.4 = ((f32[1,2,128]{1,0,2:T(1,128)}), f32[1,2,128]{1,0,2:T(1,128)S(1)}, u32[]{:S(2)}, u32[]{:S(2)}) async-start(f32[1,2,128]{1,0,2:T(1,128)} %copy.104), calls=%async_computation.4 | async-start | bytes 131072 | tf_op jit(solution)/shard_map/all_to_all | solution.py:84
  197.4 7.4 %all-to-all-done.4 = f32[1,2,128]{1,0,2:T(1,128)S(1)} async-done(((f32[1,2,128]{1,0,2:T(1,128)}), f32[1,2,128]{1,0,2:T(1,128)S(1)}, u32[]{:S(2)}, u32[]{:S(2)}) %all-to-all-start.4) | async-done | bytes 1056 | tf_op jit(solution)/shard_map/all_to_all | solution.py:84
  204.8 3.6 %all-to-all-start.1 = ((f32[1,2,128,512]{3,1,0,2:T(2,128)}), f32[1,2,128,512]{3,1,0,2:T(2,128)S(1)}, u32[]{:S(2)}, u32[]{:S(2)}) async-start(f32[1,2,128,512]{3,1,0,2:T(2,128)} %copy.93), calls=%async_computation.1 | async-start | bytes 1048576 | tf_op jit(solution)/shard_map/all_to_all | solution.py:83
  208.7 11.3 %all-to-all-done.1 = f32[1,2,128,512]{3,1,0,2:T(2,128)S(1)} async-done(((f32[1,2,128,512]{3,1,0,2:T(2,128)}), f32[1,2,128,512]{3,1,0,2:T(2,128)S(1)}, u32[]{:S(2)}, u32[]{:S(2)}) %all-to-all-start.1) | async-done | bytes 524320 | tf_op jit(solution)/shard_map/all_to_all | solution.py:83
  220.0 3.6 %all-to-all-start.3 = ((f32[1,2,128,512]{3,1,0,2:T(2,128)}), f32[1,2,128,512]{3,1,0,2:T(2,128)S(1)}, u32[]{:S(2)}, u32[]{:S(2)}) async-start(f32[1,2,128,512]{3,1,0,2:T(2,128)} %copy.100), calls=%async_computation.3 | async-start | bytes 1048576 | tf_op jit(solution)/shard_map/all_to_all | solution.py:83
  224.4 9.8 %all-to-all-done.3 = f32[1,2,128,512]{3,1,0,2:T(2,128)S(1)} async-done(((f32[1,2,128,512]{3,1,0,2:T(2,128)}), f32[1,2,128,512]{3,1,0,2:T(2,128)S(1)}, u32[]{:S(2)}, u32[]{:S(2)}) %all-to-all-start.3) | async-done | bytes 524320 | tf_op jit(solution)/shard_map/all_to_all | solution.py:83
  234.1 3.6 %all-to-all-start.5 = ((f32[1,2,128,512]{3,1,0,2:T(2,128)}), f32[1,2,128,512]{3,1,0,2:T(2,128)S(1)}, u32[]{:S(2)}, u32[]{:S(2)}) async-start(f32[1,2,128,512]{3,1,0,2:T(2,128)} %copy.107), calls=%async_computation.5 | async-start | bytes 1048576 | tf_op jit(solution)/shard_map/all_to_all | solution.py:83
  238.3 9.4 %all-to-all-done.5 = f32[1,2,128,512]{3,1,0,2:T(2,128)S(1)} async-done(((f32[1,2,128,512]{3,1,0,2:T(2,128)}), f32[1,2,128,512]{3,1,0,2:T(2,128)S(1)}, u32[]{:S(2)}, u32[]{:S(2)}) %all-to-all-start.5) | async-done | bytes 524320 | tf_op jit(solution)/shard_map/all_to_all | solution.py:83
  247.8 3.6 %all-to-all-start.7 = ((f32[1,2,128,512]{3,1,0,2:T(2,128)}), f32[1,2,128,512]{3,1,0,2:T(2,128)S(1)}, u32[]{:S(2)}, u32[]{:S(2)}) async-start(f32[1,2,128,512]{3,1,0,2:T(2,128)} %copy.114), calls=%async_computation.7 | async-start | bytes 1048576 | tf_op jit(solution)/shard_map/all_to_all | solution.py:83
  252.5 9.0 %all-to-all-done.7 = f32[1,2,128,512]{3,1,0,2:T(2,128)S(1)} async-done(((f32[1,2,128,512]{3,1,0,2:T(2,128)}), f32[1,2,128,512]{3,1,0,2:T(2,128)S(1)}, u32[]{:S(2)}, u32[]{:S(2)}) %all-to-all-start.7) | async-done | bytes 524320 | tf_op jit(solution)/shard_map/all_to_all | solution.py:83
  (188 shorter events, 50.4 us)
Async XLA Ops:
  6.5 33.5 %copy-start.47 = (s32[2]{0:T(128)S(1)}, s32[2]{0:T(128)}, u32[]{:S(2)}) copy-start(s32[2]{0:T(128)} %param.8) | copy-start | bytes 28
  8.8 85.3 %copy-start = (bf16[2,1536,576]{1,2,0:T(8,128)(2,1)S(1)}, bf16[2,1536,576]{1,2,0:T(8,128)(2,1)}, u32[]{:S(2)}) copy-start(bf16[2,1536,576]{1,2,0:T(8,128)(2,1)} %param.6) | copy-start | bytes 10616836
  130.2 14.9 %slice-start = ((bf16[4,2,576]{2,1,0:T(2,128)(2,1)}), bf16[4,2,512]{2,1,0:T(2,128)(2,1)S(1)}, s32[]{:S(2)}) async-start(bf16[4,2,576]{2,1,0:T(2,128)(2,1)} %param.7), calls=%async_computation.9 | async-start | bytes 16384 | tf_op jit(solution)/shard_map/slice | solution.py:70
  134.4 33.4 %all-to-all-start.2 = ((f32[1,2,128]{1,0,2:T(1,128)}), f32[1,2,128]{1,0,2:T(1,128)}, u32[]{:S(2)}, u32[]{:S(2)}) async-start(f32[1,2,128]{1,0,2:T(1,128)} %copy.97), calls=%async_computation.2 | async-start | bytes 131072 | tf_op jit(solution)/shard_map/all_to_all | solution.py:84
  138.6 123.5 %all-gather.6.cloned.1.call-start = ((), (), s32[]{:S(2)}) async-start(), calls=%async_computation.8 | async-start | bytes 1081344 | tf_op jit(solution)/shard_map/all_gather | solution.py:92
  139.4 18.2 %copy-start.43 = (pred[4]{0:T(512)(128)(4,1)}, pred[4]{0:T(512)(128)(4,1)S(1)}, u32[]{:S(2)}) copy-start(pred[4]{0:T(512)(128)(4,1)S(1)} %iota_compare_fusion.2) | copy-start | bytes 16
  139.4 18.3 %copy-start.45 = (pred[4]{0:T(512)(128)(4,1)}, pred[4]{0:T(512)(128)(4,1)S(1)}, u32[]{:S(2)}) copy-start(pred[4]{0:T(512)(128)(4,1)S(1)} %iota_compare_fusion.3) | copy-start | bytes 16
  142.0 15.7 %copy-start.39 = (pred[4]{0:T(512)(128)(4,1)}, pred[4]{0:T(512)(128)(4,1)S(1)}, u32[]{:S(2)}) copy-start(pred[4]{0:T(512)(128)(4,1)S(1)} %iota_compare_fusion) | copy-start | bytes 16
  142.0 15.8 %copy-start.41 = (pred[4]{0:T(512)(128)(4,1)}, pred[4]{0:T(512)(128)(4,1)S(1)}, u32[]{:S(2)}) copy-start(pred[4]{0:T(512)(128)(4,1)S(1)} %iota_compare_fusion.1) | copy-start | bytes 16
  166.5 42.1 %copy-start.21 = (f32[2,8]{1,0:T(2,128)S(1)}, f32[2,8]{1,0:T(2,128)}, u32[]{:S(2)}) copy-start(f32[2,8]{1,0:T(2,128)} %copy-done.20) | copy-start | bytes 196
  166.5 42.1 %copy-start.19 = (f32[2,8]{1,0:T(2,128)S(1)}, f32[2,8]{1,0:T(2,128)}, u32[]{:S(2)}) copy-start(f32[2,8]{1,0:T(2,128)} %copy-done.18) | copy-start | bytes 196
  167.8 14.8 %all-to-all-start = ((f32[1,2,128]{1,0,2:T(1,128)}), f32[1,2,128]{1,0,2:T(1,128)S(1)}, u32[]{:S(2)}, u32[]{:S(2)}) async-start(f32[1,2,128]{1,0,2:T(1,128)} %copy.86), calls=%async_computation | async-start | bytes 131072 | tf_op jit(solution)/shard_map/all_to_all | solution.py:84
  182.6 11.1 %all-to-all-start.6 = ((f32[1,2,128]{1,0,2:T(1,128)}), f32[1,2,128]{1,0,2:T(1,128)S(1)}, u32[]{:S(2)}, u32[]{:S(2)}) async-start(f32[1,2,128]{1,0,2:T(1,128)} %copy.111), calls=%async_computation.6 | async-start | bytes 131072 | tf_op jit(solution)/shard_map/all_to_all | solution.py:84
  193.7 11.1 %all-to-all-start.4 = ((f32[1,2,128]{1,0,2:T(1,128)}), f32[1,2,128]{1,0,2:T(1,128)S(1)}, u32[]{:S(2)}, u32[]{:S(2)}) async-start(f32[1,2,128]{1,0,2:T(1,128)} %copy.104), calls=%async_computation.4 | async-start | bytes 131072 | tf_op jit(solution)/shard_map/all_to_all | solution.py:84
  204.8 15.2 %all-to-all-start.1 = ((f32[1,2,128,512]{3,1,0,2:T(2,128)}), f32[1,2,128,512]{3,1,0,2:T(2,128)S(1)}, u32[]{:S(2)}, u32[]{:S(2)}) async-start(f32[1,2,128,512]{3,1,0,2:T(2,128)} %copy.93), calls=%async_computation.1 | async-start | bytes 1048576 | tf_op jit(solution)/shard_map/all_to_all | solution.py:83
  220.0 14.1 %all-to-all-start.3 = ((f32[1,2,128,512]{3,1,0,2:T(2,128)}), f32[1,2,128,512]{3,1,0,2:T(2,128)S(1)}, u32[]{:S(2)}, u32[]{:S(2)}) async-start(f32[1,2,128,512]{3,1,0,2:T(2,128)} %copy.100), calls=%async_computation.3 | async-start | bytes 1048576 | tf_op jit(solution)/shard_map/all_to_all | solution.py:83
  224.3 27.0 %copy-start.17 = (bf16[2,4,576]{2,1,0:T(4,128)(2,1)S(1)}, bf16[2,4,576]{2,1,0:T(4,128)(2,1)}, u32[]{:S(2)}) copy-start(bf16[2,4,576]{2,1,0:T(4,128)(2,1)} %copy-done.16) | copy-start | bytes 27652
  224.3 27.0 %copy-start.38 = (f32[2,8,4]{1,2,0:T(4,128)S(1)}, f32[2,8,4]{1,2,0:T(4,128)}, u32[]{:S(2)}) copy-start(f32[2,8,4]{1,2,0:T(4,128)} %copy-done.37) | copy-start | bytes 772
  224.3 27.0 %copy-start.46 = (pred[4]{0:T(512)(128)(4,1)S(1)}, pred[4]{0:T(512)(128)(4,1)}, u32[]{:S(2)}) copy-start(pred[4]{0:T(512)(128)(4,1)} %copy-done.45) | copy-start | bytes 16
  234.1 13.7 %all-to-all-start.5 = ((f32[1,2,128,512]{3,1,0,2:T(2,128)}), f32[1,2,128,512]{3,1,0,2:T(2,128)S(1)}, u32[]{:S(2)}, u32[]{:S(2)}) async-start(f32[1,2,128,512]{3,1,0,2:T(2,128)} %copy.107), calls=%async_computation.5 | async-start | bytes 1048576 | tf_op jit(solution)/shard_map/all_to_all | solution.py:83
  238.0 14.2 %copy-start.36 = (f32[2,8,4]{1,2,0:T(4,128)S(1)}, f32[2,8,4]{1,2,0:T(4,128)}, u32[]{:S(2)}) copy-start(f32[2,8,4]{1,2,0:T(4,128)} %copy-done.35) | copy-start | bytes 772
  238.3 23.4 %copy-start.32 = (f32[2,8,4]{1,2,0:T(4,128)S(1)}, f32[2,8,4]{1,2,0:T(4,128)}, u32[]{:S(2)}) copy-start(f32[2,8,4]{1,2,0:T(4,128)} %copy-done.31) | copy-start | bytes 772
  238.3 23.4 %copy-start.40 = (pred[4]{0:T(512)(128)(4,1)S(1)}, pred[4]{0:T(512)(128)(4,1)}, u32[]{:S(2)}) copy-start(pred[4]{0:T(512)(128)(4,1)} %copy-done.39) | copy-start | bytes 16
  247.8 13.7 %all-to-all-start.7 = ((f32[1,2,128,512]{3,1,0,2:T(2,128)}), f32[1,2,128,512]{3,1,0,2:T(2,128)S(1)}, u32[]{:S(2)}, u32[]{:S(2)}) async-start(f32[1,2,128,512]{3,1,0,2:T(2,128)} %copy.114), calls=%async_computation.7 | async-start | bytes 1048576 | tf_op jit(solution)/shard_map/all_to_all | solution.py:83
  (34 other events, 162.4 us)
Sparse Core Ops, SparseCore 0:
  141.5 66.3 all-gather.5
where the time goes:
time: 273 us; the launch traced here: 271 us
  blocking collectives  99.9 us (37%)
  waiting for transfers between devices  61.5 us (23%)
  starting transfers between devices  32.9 us (12%)
  local copies, waits for them, and re-layouts  26.9 us (10%)
  matrix products  22.9 us (8%)
  between operations  14.1 us (5%)
  other arithmetic  12.9 us (5%)
    all_gather x4, blocking collectives, body(): present = lax.all_gather(query_ready[current], 'ctx', axis=1, tiled=True)  99.9 us
    all_to_all x4, waiting for transfers between devices, body(): lax.all_to_all(parted[None], 'ctx', split_axis=2, concat_axis=0, tiled=True)  39.5 us
    all_to_all x4, waiting for transfers between devices, body(): lax.all_to_all(spread[None], 'ctx', split_axis=2, concat_axis=0, tiled=True)  21.5 us
    all_to_all x4, starting transfers between devices, body(): lax.all_to_all(spread[None], 'ctx', split_axis=2, concat_axis=0, tiled=True)  18.4 us
    all_to_all x4, starting transfers between devices, body(): lax.all_to_all(parted[None], 'ctx', split_axis=2, concat_axis=0, tiled=True)  14.3 us
    dot_general x8, matrix products, shard_partial(): jnp.einsum('bhc,bkc->bhk', present, key_rows, preferred_element_type=jnp....  11 us
    dot_general x8, matrix products, shard_partial(): jnp.einsum('bhk,bkl->bhl', weights.astype(jnp.bfloat16), key_rows[..., :L...  10.4 us
    all_gather x4, local copies, waits for them, and re-layouts, body(): present = lax.all_gather(query_ready[current], 'ctx', axis=1, tiled=True)  7.58 us
  transfers between devices with their start and end apart: 9, of which 7 were waited for; matrix products, arithmetic and copies ran while one was open for 12% of the time, Pallas kernels for 0%

commit v1 on v0

v1 whole, which is shorter than its diff:
```python
import jax
import jax.numpy as jnp
from jax import lax
from jax.experimental import pallas as pl
from jax.experimental.pallas import tpu as pltpu
from jax.sharding import PartitionSpec as P

LAT = 512
ROPE = 64
HALF = 32
NOPE = 128
SCALE = (NOPE + ROPE) ** (-0.5)
LOG2E = 1.4426950408889634
FLOOR = -1e30
F32 = jnp.float32
BF16 = jnp.bfloat16
NT = (((1,), (1,)), ((), ()))


def vmem():
    return pl.BlockSpec(memory_space=pltpu.VMEM)


def smem():
    return pl.BlockSpec(memory_space=pltpu.SMEM)


def swap_halves(x):
    lane = lax.broadcasted_iota(jnp.int32, x.shape, x.ndim - 1)
    width = x.shape[-1]
    ahead = pltpu.roll(x, width - HALF, x.ndim - 1)
    behind = pltpu.roll(x, HALF, x.ndim - 1)
    return jnp.where(lane % ROPE < HALF, ahead, behind)


def pack_kernel(q_ref, out_ref):
    steps, rows, heads, _ = q_ref.shape
    parts = []
    rotary = []
    for r in range(rows):
        for s in range(steps):
            block = q_ref[s, r].astype(F32)
            parts.append(block[:, :LAT])
            rotary.append(block[:, LAT:])
    parts.append(jnp.concatenate(rotary, axis=1))
    whole = jnp.concatenate(parts, axis=0).astype(BF16)
    for d in range(out_ref.shape[0]):
        out_ref[d] = whole


def pack_queries(queries, shards):
    steps, rows, heads, _ = queries.shape
    count = steps * rows * heads
    return pl.pallas_call(
        pack_kernel,
        out_shape=jax.ShapeDtypeStruct((shards, count + heads, LAT), BF16),
        in_specs=[vmem()],
        out_specs=vmem(),
        name="pack_queries",
    )(queries)


def fresh_kernel(q_ref, new_ref, cos_ref, sin_ref, mixed_ref, lse_ref):
    steps, rows, heads, _ = q_ref.shape
    count = rows * steps * heads
    keys = rows * steps
    cos = cos_ref[...]
    sin = sin_ref[...]
    q_lat = []
    q_rot = []
    key_lat = []
    key_rot = []
    for r in range(rows):
        for s in range(steps):
            row_cos = cos[r * steps + s : r * steps + s + 1]
            row_sin = sin[r * steps + s : r * steps + s + 1]
            block = q_ref[s, r].astype(F32)
            q_lat.append(block[:, :LAT])
            wide = jnp.concatenate([block[:, LAT:], block[:, LAT:]], axis=1)
            q_rot.append(wide * row_cos + swap_halves(wide) * row_sin)
            key = new_ref[s, r : r + 1].astype(F32)
            key_lat.append(key[:, :LAT])
            wide = jnp.concatenate([key[:, LAT:], key[:, LAT:]], axis=1)
            wide = jnp.broadcast_to(wide, (8, 2 * ROPE))
            wide = wide * row_cos + swap_halves(wide) * row_sin
            key_rot.append(wide[:1])
    q_lat = jnp.concatenate(q_lat, axis=0).astype(BF16)
    q_rot = jnp.concatenate(q_rot, axis=0)[:, :ROPE].astype(BF16)
    pad = jnp.zeros((128 - keys, LAT), F32)
    key_lat = jnp.concatenate(key_lat + [pad], axis=0).astype(BF16)
    key_rot = jnp.concatenate(key_rot + [pad[:, : 2 * ROPE]], axis=0)[:, :ROPE].astype(BF16)
    scores = lax.dot_general(q_lat, key_lat, NT, preferred_element_type=F32)
    scores += lax.dot_general(q_rot, key_rot, NT, preferred_element_type=F32)
    scores *= SCALE
    query = lax.broadcasted_iota(jnp.int32, (count, 128), 0) // heads
    key = lax.broadcasted_iota(jnp.int32, (count, 128), 1)
    valid = (key <= query) & (key // steps == query // steps)
    scores = jnp.where(valid, scores, FLOOR)
    top = jnp.max(scores, axis=1, keepdims=True)
    weights = jnp.where(valid, jnp.exp(scores - top), 0.0)
    total = jnp.sum(weights, axis=1, keepdims=True)
    mixed = jnp.dot(weights.astype(BF16), key_lat, preferred_element_type=F32)
    mixed_ref[...] = mixed / total
    lse_ref[...] = as_rows((top + jnp.log(total)).reshape(rows, steps * heads, 1))


def as_rows(column):
    n, span, _ = column.shape
    row = lax.broadcasted_iota(jnp.int32, (n, span, 128), 1)
    lane = lax.broadcasted_iota(jnp.int32, (n, span, 128), 2)
    return jnp.sum(jnp.where(row == lane, column, 0.0), axis=1)


def fresh_part(queries, new_latent, cos, sin):
    steps, rows, heads, _ = queries.shape
    count = steps * rows * heads
    return pl.pallas_call(
        fresh_kernel,
        out_shape=(
            jax.ShapeDtypeStruct((count, LAT), F32),
            jax.ShapeDtypeStruct((rows, 128), F32),
        ),
        in_specs=[vmem()] * 4,
        out_specs=(vmem(), vmem()),
        name="fresh_part",
    )(queries, new_latent, cos, sin)


def attend_kernel(live_ref, q_ref, cos_ref, sin_ref, cache_ref, out_ref, keys, q_scr, sems):
    rows, span, _ = cache_ref.shape
    shards, stride, _ = q_ref.shape
    heads = 8
    count = stride - heads
    per_row = count // rows
    steps = per_row // heads
    copies = [
        pltpu.make_async_copy(cache_ref.at[r], keys.at[r], sems.at[r]) for r in range(rows)
    ]
    for copy in copies:
        copy.start()
    packed = q_ref[:, count:, :].astype(F32).reshape(shards * heads, LAT)
    lse_rows = []
    for r in range(rows):
        q_scr[:, :LAT] = q_ref[:, r * per_row : (r + 1) * per_row, :].reshape(
            shards * per_row, LAT
        )
        width = steps * ROPE
        part = packed[:, r * width : (r + 1) * width]
        turned = part * cos_ref[r : r + 1] + swap_halves(part) * sin_ref[r : r + 1]
        turned = jnp.stack(
            [
                turned[:, s * ROPE : (s + 1) * ROPE].reshape(shards, heads, ROPE)
                for s in range(steps)
            ],
            axis=1,
        ).reshape(shards * per_row, ROPE)
        q_scr[:, LAT:] = turned.astype(BF16)
        copies[r].wait()
        scores = lax.dot_general(q_scr[...], keys[r], NT, preferred_element_type=F32)
        slot = lax.broadcasted_iota(jnp.int32, scores.shape, 1)
        scores = jnp.where(slot < live_ref[r], scores, FLOOR)
        top = jnp.max(scores, axis=1, keepdims=True)
        weights = jnp.exp2((scores - top) * (SCALE * LOG2E))
        total = jnp.sum(weights, axis=1, keepdims=True)
        mixed = jnp.dot(weights.astype(BF16), keys[r, :, :LAT], preferred_element_type=F32)
        mixed = mixed * (1.0 / total)
        out_ref[:, r * per_row : (r + 1) * per_row, :] = (
            mixed.astype(BF16).reshape(shards, per_row, LAT)
        )
        lse = jnp.where(live_ref[r] > 0, top * SCALE + jnp.log(total), FLOOR)
        lse_rows.append(as_rows(lse.reshape(shards, per_row, 1)))
    tail = jnp.zeros((shards, heads, 128), F32)
    which = lax.broadcasted_iota(jnp.int32, tail.shape, 1)
    for r in range(rows):
        rest = lse_rows[r]
        for term in range(3):
            piece = rest.astype(BF16).astype(F32)
            tail = jnp.where(which == 3 * r + term, piece[:, None, :], tail)
            rest = rest - piece
    tail = jnp.concatenate([tail, jnp.zeros((shards, heads, LAT - 128), F32)], axis=2)
    out_ref[:, count:, :] = tail.astype(BF16)


def attend(live, gathered, cos, sin, cache):
    rows, span, width = cache.shape
    shards, stride, _ = gathered.shape
    per_row = (stride - 8) // rows
    return pl.pallas_call(
        attend_kernel,
        out_shape=jax.ShapeDtypeStruct(gathered.shape, BF16),
        in_specs=[smem(), vmem(), vmem(), vmem(), pl.BlockSpec(memory_space=pl.ANY)],
        out_specs=vmem(),
        scratch_shapes=[
            pltpu.VMEM((rows, span, width), BF16),
            pltpu.VMEM((shards * per_row, width), BF16),
            pltpu.SemaphoreType.DMA((rows,)),
        ],
        compiler_params=pltpu.CompilerParams(vmem_limit_bytes=40 * 1024 * 1024),
        cost_estimate=pl.CostEstimate(
            flops=2 * rows * shards * per_row * span * (width + LAT),
            bytes_accessed=cache.size * 2 + gathered.size * 4,
            transcendentals=rows * shards * per_row * span,
        ),
        name="attend",
    )(live, gathered, cos, sin, cache)


def merge_kernel(place_ref, got_ref, fresh_ref, fresh_lse_ref, own_ref, other_ref, out_ref, up):
    shards, stride, _ = got_ref.shape
    steps, rows, heads, _ = out_ref.shape
    count = stride - heads
    per_row = count // rows
    blocks, _, depth, _ = own_ref.shape
    for source, ref in enumerate((own_ref, other_ref)):
        for b in range(blocks):
            start = pl.multiple_of(place_ref[source * blocks + b] * depth, depth)
            up[:, pl.ds(start, depth), :] = ref[b]
    tail = got_ref[:, count:, :128].astype(F32)
    sub = lax.broadcasted_iota(jnp.int32, (per_row, 128), 0)
    lane = lax.broadcasted_iota(jnp.int32, (per_row, 128), 1)
    eye = sub == lane

    def column(row):
        return jnp.sum(jnp.where(eye, row, 0.0), axis=1, keepdims=True)

    merged = []
    for r in range(rows):
        spread = tail[:, 3 * r] + tail[:, 3 * r + 1] + tail[:, 3 * r + 2]
        own = fresh_lse_ref[r : r + 1]
        top = jnp.maximum(jnp.max(spread, axis=0, keepdims=True), own)
        factor = jnp.exp(spread - top)
        own_factor = jnp.exp(own - top)
        scale = 1.0 / (jnp.sum(factor, axis=0, keepdims=True) + own_factor)
        factor = factor * scale
        first = r * per_row
        total = column(own_factor * scale) * fresh_ref[first : first + per_row]
        for d in range(shards):
            piece = got_ref[d, first : first + per_row, :].astype(F32)
            total += column(factor[d : d + 1]) * piece
        merged.append(total)
    latent = jnp.concatenate(merged, axis=0).astype(BF16)
    head = lax.broadcasted_iota(jnp.int32, (count, 128), 0) % heads
    result = jnp.zeros((count, 128), F32)
    for h in range(heads):
        product = jnp.dot(latent, up[h], preferred_element_type=F32)
        result = jnp.where(head == h, product, result)
    for r in range(rows):
        for s in range(steps):
            first = (r * steps + s) * heads
            out_ref[s, r] = result[first : first + heads]


def merge(place, got, fresh, fresh_lse, own, other, steps, rows):
    blocks, heads, depth, width = own.shape
    return pl.pallas_call(
        merge_kernel,
        out_shape=jax.ShapeDtypeStruct((steps, rows, heads, width), F32),
        in_specs=[smem()] + [vmem()] * 5,
        out_specs=vmem(),
        scratch_shapes=[pltpu.VMEM((heads, 2 * blocks * depth, width), BF16)],
        compiler_params=pltpu.CompilerParams(vmem_limit_bytes=16 * 1024 * 1024),
        name="merge",
    )(place, got, fresh, fresh_lse, own, other)


def body(queries, latent_cache, new_latent, lengths, value_up):
    steps, rows, heads, _ = queries.shape
    shards = lax.axis_size("ctx")
    lines = lax.axis_size("dp")
    chips = lines // 2
    span = latent_cache.shape[1]

    def from_line(x, reach):
        pairs = []
        for line in range(lines):
            z, core = line // 2, line % 2
            sign = 1 - 2 * core
            pairs.append((((z + sign * reach) % chips) * 2 + core, line))
        return lax.ppermute(x, "dp", pairs)

    packed = pack_queries(queries, shards)
    gathered = lax.all_to_all(packed, "ctx", 0, 0, tiled=True)

    held = value_up[None]
    reach = chips // 2
    while reach >= 1:
        held = jnp.concatenate([held, from_line(held, reach)], axis=0)
        reach //= 2
    other = lax.ppermute(held, "dp", [(i, i ^ 1) for i in range(lines)])

    line = lax.axis_index("dp")
    z, core = line // 2, line % 2
    sign = 1 - 2 * core
    index = jnp.arange(chips, dtype=jnp.int32)
    ahead = jnp.zeros_like(index)
    reach, bit = chips // 2, 0
    while reach >= 1:
        ahead += ((index >> bit) & 1) * reach
        reach, bit = reach // 2, bit + 1
    place = jnp.concatenate(
        [
            ((z + sign * ahead) % chips) * 2 + core,
            ((z - sign * ahead) % chips) * 2 + (1 - core),
        ]
    ).astype(jnp.int32)

    pair_index = jnp.arange(HALF, dtype=F32)
    frequency = jnp.power(F32(10000.0), -2.0 * pair_index / ROPE)
    positions = (lengths[:, None] + jnp.arange(steps, dtype=jnp.int32)[None, :]).astype(F32)
    angles = positions[..., None] * frequency
    cosine = jnp.cos(angles)
    sine = jnp.sin(angles)
    cos = jnp.concatenate([cosine, cosine], axis=-1)
    sin = jnp.concatenate([-sine, sine], axis=-1)
    cos_pair = jnp.concatenate([cos, cos], axis=-1).reshape(rows * steps, 2 * ROPE)
    sin_pair = jnp.concatenate([sin, sin], axis=-1).reshape(rows * steps, 2 * ROPE)
    cos = cos.reshape(rows, steps * ROPE)
    sin = sin.reshape(rows, steps * ROPE)

    fresh, fresh_lse = fresh_part(queries, new_latent, cos_pair, sin_pair)
    live = jnp.clip(lengths - lax.axis_index("ctx") * span, 0, span)
    partial = attend(live, gathered, cos, sin, latent_cache)
    got = lax.all_to_all(partial, "ctx", 0, 0, tiled=True)
    return merge(place, got, fresh, fresh_lse, held, other, steps, rows)


def solution(mesh):
    placed = (
        P(None, "dp", "ctx", None),
        P("dp", "ctx", None),
        P(None, "dp", None),
        P("dp"),
        P("ctx", "dp", None),
    )
    return jax.shard_map(
        body, mesh=mesh, in_specs=placed, out_specs=P(None, "dp", "ctx", None), check_vma=False
    )
```

time: 273 us -> 84.9 us (0.31)
  the two profiles are of different devices: /device:TPU:256 before, /device:TPU:1 now
where the time goes in v1:
time: 84.9 us; the launch traced here: 83.7 us
  starting transfers between devices  52.4 us (62%)
  Pallas kernels  13.9 us (16%)
  local copies, waits for them, and re-layouts  9.99 us (12%)
  waiting for transfers between devices  5.98 us (7%)
  other arithmetic  1.23 us (1%)
    ppermute x4, starting transfers between devices, from_line(): return lax.ppermute(x, 'dp', pairs)  29.2 us
    unnamed x15, local copies, waits for them, and re-layouts  9.71 us
    ppermute x1, starting transfers between devices, body(): other = lax.ppermute(held, 'dp', [(i, i ^ 1) for i in range(lines)])  8.83 us
    pallas_call x1, Pallas kernels, attend(): pl.pallas_call(attend_kernel, out_shape=jax.ShapeDtypeStruct(gathered.sha...  8 us
    all_to_all x1, starting transfers between devices, body(): gathered = lax.all_to_all(packed, 'ctx', 0, 0, tiled=True)  7.72 us
    all_to_all x1, starting transfers between devices, body(): got = lax.all_to_all(partial, 'ctx', 0, 0, tiled=True)  6.66 us
    ppermute x4, waiting for transfers between devices, from_line(): return lax.ppermute(x, 'dp', pairs)  5.97 us
    pallas_call x1, Pallas kernels, fresh_part(): pl.pallas_call(fresh_kernel, out_shape=(jax.ShapeDtypeStruct((count, LAT)...  2.08 us
  transfers between devices with their start and end apart: 7, of which 2 were waited for; matrix products, arithmetic and copies ran while one was open for 9% of the time, Pallas kernels for 12%

profile of v1, /device:TPU:1, one launch (start us, length us, event | category | flops | bytes accessed | tf_op | source)
XLA Modules:
  0.0 83.7 jit_solution(862992785116435460)
XLA Ops:
  0.0 2.0 %pack_queries.1 = bf16[16,72,512]{2,1,0:T(8,128)(2,1)} custom-call(bf16[4,2,8,576]{3,2,1,0:T(8,128)(2,1)} %q_ref.3), custom_call_target="tpu_custom_call" | custom-call | tf_op jit(solution)/shard_map/pack_queries/pallas_call | solution.py:54
  2.0 7.7 %all-to-all-start = ((bf16[16,72,512]{2,1,0:T(8,128)(2,1)}), bf16[16,72,512]{2,1,0:T(8,128)(2,1)S(1)}, u32[]{:S(2)}, u32[]{:S(2)}) async-start(bf16[16,72,512]{2,1,0:T(8,128)(2,1)} %pack_queries.1), calls=%async_computation | async-start | bytes 2359296 | tf_op jit(solution)/shard_map/all_to_all | solution.py:282
  9.7 15.4 %collective-permute-start = (bf16[1,8,16,128]{3,2,1,0:T(8,128)(2,1)S(1)}, bf16[1,8,16,128]{3,2,1,0:T(8,128)(2,1)S(1)}, u32[]{:S(2)}, u32[]{:S(2)}) collective-permute-start(bf16[1,8,16,128]{3,2,1,0:T(8,128)(2,1)S(1)} %bitcast.2), channel_id=1, source_target_pairs={{256,0},{272,16},{288,32},{304,48},{320,64},{336,80},{352,96},{368... | collective-permute-start | bytes 98312 | tf_op jit(solution)/shard_map/ppermute | solution.py:279
  25.3 0.1 fusion.18
  25.4 0.1 convert_element_type.12
  25.5 1.0 %collective-permute-done = bf16[1,8,16,128]{3,2,1,0:T(8,128)(2,1)S(1)} collective-permute-done((bf16[1,8,16,128]{3,2,1,0:T(8,128)(2,1)S(1)}, bf16[1,8,16,128]{3,2,1,0:T(8,128)(2,1)S(1)}, u32[]{:S(2)}, u32[]{:S(2)}) %collective-permute-start) | collective-permute-done | bytes 32800 | tf_op jit(solution)/shard_map/ppermute | solution.py:279
  26.6 5.3 %collective-permute-start.1 = (bf16[2,8,16,128]{3,2,1,0:T(8,128)(2,1)S(1)}, bf16[2,8,16,128]{3,2,1,0:T(8,128)(2,1)S(1)}, u32[]{:S(2)}, u32[]{:S(2)}) collective-permute-start(bf16[2,8,16,128]{3,2,1,0:T(8,128)(2,1)S(1)} %pad_maximum_fusion.2), channel_id=1, source_target_pairs={{128,0},{400,16},{160,32},{432,48},{192,64},{464,80},{224,96},{496... | collective-permute-start | bytes 196616 | tf_op jit(solution)/shard_map/ppermute | solution.py:279
  32.0 0.1 reshape.63.cos_ref
  32.1 0.1 reshape.64.sin_ref
  32.2 6.0 %copy.6.cache_ref = bf16[2,1536,576]{2,1,0:T(8,128)(2,1)} copy(bf16[2,1536,576]{1,2,0:T(8,128)(2,1)} %param.6) | data formatting | bytes 7077888 | tf_op args[1]
  38.1 5.1 %collective-permute-start.2 = (bf16[4,8,16,128]{3,2,1,0:T(8,128)(2,1)S(1)}, bf16[4,8,16,128]{3,2,1,0:T(8,128)(2,1)S(1)}, u32[]{:S(2)}, u32[]{:S(2)}) collective-permute-start(bf16[4,8,16,128]{3,2,1,0:T(8,128)(2,1)S(1)} %pad_maximum_fusion.1), channel_id=1, source_target_pairs={{64,0},{464,16},{96,32},{496,48},{128,64},{16,80},{160,96},{48,112... | collective-permute-start | bytes 393224 | tf_op jit(solution)/shard_map/ppermute | solution.py:279
  43.3 2.1 %copy-done = bf16[2,1536,576]{2,1,0:T(8,128)(2,1)S(1)} copy-done((bf16[2,1536,576]{2,1,0:T(8,128)(2,1)S(1)}, bf16[2,1536,576]{2,1,0:T(8,128)(2,1)}, u32[]{:S(2)}) %copy-start) | copy-done | bytes 3538968
  45.4 8.0 %attend.1 = bf16[16,72,512]{2,1,0:T(8,128)(2,1)} custom-call(s32[2]{0:T(128)S(1)} %subtract_clamp_fusion.live_ref, bf16[16,72,512]{2,1,0:T(8,128)(2,1)S(1)} %all-to-all-done.q_ref, f32[2,256]{1,0:T(2,128)S(1)} %reshape.63.cos_ref, f32[2,256]{1,0:T(2,128)S(1)} %reshape.64.sin_ref, bf16[2,1536,576]{2,1,0:T(8,128)(2,1)S(1)} %copy-done), custom_call_target="tpu_custom_call" | custom-call | flops 3422552064 | bytes 5898240 | tf_op jit(solution)/shard_map/attend/pallas_call | solution.py:188
  53.4 6.7 %all-to-all-start.1 = ((bf16[16,72,512]{2,1,0:T(8,128)(2,1)}), bf16[16,72,512]{2,1,0:T(8,128)(2,1)S(1)}, u32[]{:S(2)}, u32[]{:S(2)}) async-start(bf16[16,72,512]{2,1,0:T(8,128)(2,1)} %attend.1), calls=%async_computation.1 | async-start | bytes 2359296 | tf_op jit(solution)/shard_map/all_to_all | solution.py:323
  60.1 3.3 %collective-permute-start.3 = (bf16[8,8,16,128]{3,2,1,0:T(8,128)(2,1)S(1)}, bf16[8,8,16,128]{3,2,1,0:T(8,128)(2,1)S(1)}, u32[]{:S(2)}, u32[]{:S(2)}) collective-permute-start(bf16[8,8,16,128]{3,2,1,0:T(8,128)(2,1)S(1)} %pad_maximum_fusion), channel_id=1, source_target_pairs={{32,0},{496,16},{64,32},{16,48},{96,64},{48,80},{128,96},{80,112},... | collective-permute-start | bytes 786440 | tf_op jit(solution)/shard_map/ppermute | solution.py:279
  63.5 4.9 %collective-permute-done.3 = bf16[8,8,16,128]{3,2,1,0:T(8,128)(2,1)S(1)} collective-permute-done((bf16[8,8,16,128]{3,2,1,0:T(8,128)(2,1)S(1)}, bf16[8,8,16,128]{3,2,1,0:T(8,128)(2,1)S(1)}, u32[]{:S(2)}, u32[]{:S(2)}) %collective-permute-start.3) | collective-permute-done | bytes 262176 | tf_op jit(solution)/shard_map/ppermute | solution.py:279
  68.5 8.8 %collective-permute-start.4 = (bf16[16,8,16,128]{3,2,1,0:T(8,128)(2,1)S(1)}, bf16[16,8,16,128]{3,2,1,0:T(8,128)(2,1)S(1)}, u32[]{:S(2)}, u32[]{:S(2)}) collective-permute-start(bf16[16,8,16,128]{3,2,1,0:T(8,128)(2,1)S(1)} %constant_dynamic-update-slice_fusion.own_ref), channel_id=1, source_target_pairs={{0,16},{16,0},{32,48},{48,32},{64,80},{80,64},{96,112},{112,96},{1... | collective-permute-start | bytes 1572872 | tf_op jit(solution)/shard_map/ppermute | solution.py:289
  77.3 0.1 fusion
  77.4 0.7 pad_maximum_fusion.5
  78.1 2.1 %fresh_part.1 = (f32[64,512]{1,0:T(8,128)}, f32[2,128]{1,0:T(2,128)}) custom-call(bf16[4,2,8,576]{3,2,1,0:T(8,128)(2,1)} %q_ref.3, bf16[4,2,576]{2,1,0:T(2,128)(2,1)} %new_ref.1, f32[8,128]{1,0:T(8,128)} %get-tuple-element.19.cos_ref, f32[8,128]{1,0:T(8,128)} %get-tuple-element.20.sin_ref), custom_call_target="tpu_custom_call" | custom-call | tf_op jit(solution)/shard_map/fresh_part/pallas_call | solution.py:117
  80.2 0.1 pad_add_fusion.place_ref
  80.3 0.9 %copy-done.1 = f32[64,512]{1,0:T(8,128)S(1)} copy-done((f32[64,512]{1,0:T(8,128)S(1)}, f32[64,512]{1,0:T(8,128)}, u32[]{:S(2)}) %copy-start.1) | copy-done | bytes 131096
  81.2 0.7 copy-done.2
  81.9 1.8 %merge.1 = f32[4,2,8,128]{3,2,1,0:T(8,128)} custom-call(s32[32]{0:T(128)S(1)} %pad_add_fusion.place_ref, bf16[16,72,512]{2,1,0:T(8,128)(2,1)S(1)} %all-to-all-done.1.got_ref, f32[64,512]{1,0:T(8,128)S(1)} %copy-done.1, f32[2,128]{1,0:T(2,128)S(1)} %copy-done.2, bf16[16,8,16,128]{3,2,1,0:T(8,128)(2,1)S(1)} %constant_dynamic-update-slice_fusion.own_ref, ...), custom_call_target="tpu_custom_call" | custom-call | tf_op jit(solution)/shard_map/merge/pallas_call | solution.py:255
  (25 shorter events, 0.3 us)
Async XLA Ops:
  2.0 7.7 %copy-start.3 = (bf16[8,16,128]{2,1,0:T(8,128)(2,1)S(1)}, bf16[8,16,128]{2,1,0:T(8,128)(2,1)}, u32[]{:S(2)}) copy-start(bf16[8,16,128]{2,1,0:T(8,128)(2,1)} %param.9) | copy-start | bytes 98308
  2.0 23.2 %copy-start.4 = (s32[2]{0:T(128)S(1)}, s32[2]{0:T(128)}, u32[]{:S(2)}) copy-start(s32[2]{0:T(128)} %param.8) | copy-start | bytes 28
  2.0 41.3 %all-to-all-start = ((bf16[16,72,512]{2,1,0:T(8,128)(2,1)}), bf16[16,72,512]{2,1,0:T(8,128)(2,1)S(1)}, u32[]{:S(2)}, u32[]{:S(2)}) async-start(bf16[16,72,512]{2,1,0:T(8,128)(2,1)} %pack_queries.1), calls=%async_computation | async-start | bytes 2359296 | tf_op jit(solution)/shard_map/all_to_all | solution.py:282
  9.7 16.8 %collective-permute-start = (bf16[1,8,16,128]{3,2,1,0:T(8,128)(2,1)S(1)}, bf16[1,8,16,128]{3,2,1,0:T(8,128)(2,1)S(1)}, u32[]{:S(2)}, u32[]{:S(2)}) collective-permute-start(bf16[1,8,16,128]{3,2,1,0:T(8,128)(2,1)S(1)} %bitcast.2), channel_id=1, source_target_pairs={{256,0},{272,16},{288,32},{304,48},{320,64},{336,80},{352,96},{368... | collective-permute-start | bytes 98312 | tf_op jit(solution)/shard_map/ppermute | solution.py:279
  26.6 11.6 %collective-permute-start.1 = (bf16[2,8,16,128]{3,2,1,0:T(8,128)(2,1)S(1)}, bf16[2,8,16,128]{3,2,1,0:T(8,128)(2,1)S(1)}, u32[]{:S(2)}, u32[]{:S(2)}) collective-permute-start(bf16[2,8,16,128]{3,2,1,0:T(8,128)(2,1)S(1)} %pad_maximum_fusion.2), channel_id=1, source_target_pairs={{128,0},{400,16},{160,32},{432,48},{192,64},{464,80},{224,96},{496... | collective-permute-start | bytes 196616 | tf_op jit(solution)/shard_map/ppermute | solution.py:279
  38.1 21.9 %collective-permute-start.2 = (bf16[4,8,16,128]{3,2,1,0:T(8,128)(2,1)S(1)}, bf16[4,8,16,128]{3,2,1,0:T(8,128)(2,1)S(1)}, u32[]{:S(2)}, u32[]{:S(2)}) collective-permute-start(bf16[4,8,16,128]{3,2,1,0:T(8,128)(2,1)S(1)} %pad_maximum_fusion.1), channel_id=1, source_target_pairs={{64,0},{464,16},{96,32},{496,48},{128,64},{16,80},{160,96},{48,112... | collective-permute-start | bytes 393224 | tf_op jit(solution)/shard_map/ppermute | solution.py:279
  43.3 2.1 %copy-start = (bf16[2,1536,576]{2,1,0:T(8,128)(2,1)S(1)}, bf16[2,1536,576]{2,1,0:T(8,128)(2,1)}, u32[]{:S(2)}) copy-start(bf16[2,1536,576]{2,1,0:T(8,128)(2,1)} %copy.6.cache_ref) | copy-start | bytes 10616836
  53.4 26.9 %all-to-all-start.1 = ((bf16[16,72,512]{2,1,0:T(8,128)(2,1)}), bf16[16,72,512]{2,1,0:T(8,128)(2,1)S(1)}, u32[]{:S(2)}, u32[]{:S(2)}) async-start(bf16[16,72,512]{2,1,0:T(8,128)(2,1)} %attend.1), calls=%async_computation.1 | async-start | bytes 2359296 | tf_op jit(solution)/shard_map/all_to_all | solution.py:323
  60.1 8.3 %collective-permute-start.3 = (bf16[8,8,16,128]{3,2,1,0:T(8,128)(2,1)S(1)}, bf16[8,8,16,128]{3,2,1,0:T(8,128)(2,1)S(1)}, u32[]{:S(2)}, u32[]{:S(2)}) collective-permute-start(bf16[8,8,16,128]{3,2,1,0:T(8,128)(2,1)S(1)} %pad_maximum_fusion), channel_id=1, source_target_pairs={{32,0},{496,16},{64,32},{16,48},{96,64},{48,80},{128,96},{80,112},... | collective-permute-start | bytes 786440 | tf_op jit(solution)/shard_map/ppermute | solution.py:279
  68.5 11.8 %collective-permute-start.4 = (bf16[16,8,16,128]{3,2,1,0:T(8,128)(2,1)S(1)}, bf16[16,8,16,128]{3,2,1,0:T(8,128)(2,1)S(1)}, u32[]{:S(2)}, u32[]{:S(2)}) collective-permute-start(bf16[16,8,16,128]{3,2,1,0:T(8,128)(2,1)S(1)} %constant_dynamic-update-slice_fusion.own_ref), channel_id=1, source_target_pairs={{0,16},{16,0},{32,48},{48,32},{64,80},{80,64},{96,112},{112,96},{1... | collective-permute-start | bytes 1572872 | tf_op jit(solution)/shard_map/ppermute | solution.py:289
  80.3 0.9 %copy-start.1 = (f32[64,512]{1,0:T(8,128)S(1)}, f32[64,512]{1,0:T(8,128)}, u32[]{:S(2)}) copy-start(f32[64,512]{1,0:T(8,128)} %get-tuple-element.7.fresh_ref) | copy-start | bytes 393220
  81.2 0.7 copy-start.2

commit v2 on v1

v2 whole, which is shorter than its diff:
```python
import functools

import jax
import jax.numpy as jnp
from jax import lax
from jax.experimental import pallas as pl
from jax.experimental.pallas import tpu as pltpu
from jax.sharding import PartitionSpec as P

LAT = 512
ROPE = 64
HALF = 32
NOPE = 128
SCALE = (NOPE + ROPE) ** (-0.5)
LOG2E = 1.4426950408889634
FLOOR = -1e30
F32 = jnp.float32
BF16 = jnp.bfloat16
NT = (((1,), (1,)), ((), ()))


def vmem():
    return pl.BlockSpec(memory_space=pltpu.VMEM)


def smem():
    return pl.BlockSpec(memory_space=pltpu.SMEM)


def swap_halves(x):
    lane = lax.broadcasted_iota(jnp.int32, x.shape, x.ndim - 1)
    width = x.shape[-1]
    ahead = pltpu.roll(x, width - HALF, x.ndim - 1)
    behind = pltpu.roll(x, HALF, x.ndim - 1)
    return jnp.where(lane % ROPE < HALF, ahead, behind)


def pack_kernel(q_ref, out_ref):
    steps, rows, heads, _ = q_ref.shape
    parts = []
    rotary = []
    for r in range(rows):
        for s in range(steps):
            block = q_ref[s, r].astype(F32)
            parts.append(block[:, :LAT])
            rotary.append(block[:, LAT:])
    parts.append(jnp.concatenate(rotary, axis=1))
    whole = jnp.concatenate(parts, axis=0).astype(BF16)
    for d in range(out_ref.shape[0]):
        out_ref[d] = whole


def pack_queries(queries, shards):
    steps, rows, heads, _ = queries.shape
    count = steps * rows * heads
    return pl.pallas_call(
        pack_kernel,
        out_shape=jax.ShapeDtypeStruct((shards, count + heads, LAT), BF16),
        in_specs=[vmem()],
        out_specs=vmem(),
        name="pack_queries",
    )(queries)


def fresh_kernel(
    q_ref, new_ref, cos_ref, sin_ref, up_ref, mixed_ref, lse_ref, wide_cos_ref, wide_sin_ref, near_ref
):
    steps, rows, heads, _ = q_ref.shape
    count = rows * steps * heads
    keys = rows * steps
    near_ref[...] = up_ref[...]
    q_lat = []
    q_rot = []
    key_lat = []
    key_rot = []
    for r in range(rows):
        for s in range(steps):
            cos = cos_ref[r, s : s + 1]
            sin = sin_ref[r, s : s + 1]
            row_cos = jnp.concatenate([cos, cos, cos, cos], axis=1)
            row_sin = jnp.concatenate([-sin, sin, -sin, sin], axis=1)
            wide_cos_ref[r : r + 1, s * ROPE : (s + 1) * ROPE] = row_cos[:, :ROPE]
            wide_sin_ref[r : r + 1, s * ROPE : (s + 1) * ROPE] = row_sin[:, :ROPE]
            block = q_ref[s, r].astype(F32)
            q_lat.append(block[:, :LAT])
            wide = jnp.concatenate([block[:, LAT:], block[:, LAT:]], axis=1)
            q_rot.append(wide * row_cos + swap_halves(wide) * row_sin)
            key = new_ref[s, r : r + 1].astype(F32)
            key_lat.append(key[:, :LAT])
            wide = jnp.concatenate([key[:, LAT:], key[:, LAT:]], axis=1)
            wide = jnp.broadcast_to(wide, (8, 2 * ROPE))
            wide = wide * row_cos + swap_halves(wide) * row_sin
            key_rot.append(wide[:1])
    q_lat = jnp.concatenate(q_lat, axis=0).astype(BF16)
    q_rot = jnp.concatenate(q_rot, axis=0)[:, :ROPE].astype(BF16)
    pad = jnp.zeros((128 - keys, LAT), F32)
    key_lat = jnp.concatenate(key_lat + [pad], axis=0).astype(BF16)
    key_rot = jnp.concatenate(key_rot + [pad[:, : 2 * ROPE]], axis=0)[:, :ROPE].astype(BF16)
    scores = lax.dot_general(q_lat, key_lat, NT, preferred_element_type=F32)
    scores += lax.dot_general(q_rot, key_rot, NT, preferred_element_type=F32)
    scores *= SCALE
    query = lax.broadcasted_iota(jnp.int32, (count, 128), 0) // heads
    key = lax.broadcasted_iota(jnp.int32, (count, 128), 1)
    valid = (key <= query) & (key // steps == query // steps)
    scores = jnp.where(valid, scores, FLOOR)
    top = jnp.max(scores, axis=1, keepdims=True)
    weights = jnp.where(valid, jnp.exp(scores - top), 0.0)
    total = jnp.sum(weights, axis=1, keepdims=True)
    mixed = jnp.dot(weights.astype(BF16), key_lat, preferred_element_type=F32)
    mixed_ref[...] = mixed / total
    lse_ref[...] = as_rows((top + jnp.log(total)).reshape(rows, steps * heads, 1))


def as_rows(column):
    n, span, _ = column.shape
    row = lax.broadcasted_iota(jnp.int32, (n, span, 128), 1)
    lane = lax.broadcasted_iota(jnp.int32, (n, span, 128), 2)
    return jnp.sum(jnp.where(row == lane, column, 0.0), axis=1)


def fresh_part(queries, new_latent, cos, sin, value_up):
    steps, rows, heads, _ = queries.shape
    count = steps * rows * heads
    return pl.pallas_call(
        fresh_kernel,
        out_shape=(
            jax.ShapeDtypeStruct((count, LAT), F32),
            jax.ShapeDtypeStruct((rows, 128), F32),
            jax.ShapeDtypeStruct((rows, steps * ROPE), F32),
            jax.ShapeDtypeStruct((rows, steps * ROPE), F32),
            jax.ShapeDtypeStruct(value_up.shape, BF16),
        ),
        in_specs=[vmem()] * 5,
        out_specs=(vmem(),) * 5,
        cost_estimate=pl.CostEstimate(flops=10**11, bytes_accessed=0, transcendentals=0),
        name="fresh_part",
    )(queries, new_latent, cos, sin, value_up)


def attend_kernel(lengths_ref, q_ref, cos_ref, sin_ref, cache_ref, out_ref, keys_ref, q_scr, sems):
    rows, _, span = cache_ref.shape
    shards, stride, _ = q_ref.shape
    heads = 8
    count = stride - heads
    copies = [
        pltpu.make_async_copy(cache_ref.at[r], keys_ref.at[r], sems.at[r]) for r in range(rows)
    ]
    for copy in copies:
        copy.start()
    per_row = count // rows
    steps = per_row // heads
    packed = q_ref[:, count:, :].astype(F32).reshape(shards * heads, LAT)
    first_slot = lax.axis_index("ctx") * span
    scored = []
    for r in range(rows):
        live = lengths_ref[r] - first_slot
        q_scr[r, :, :LAT] = q_ref[:, r * per_row : (r + 1) * per_row, :].reshape(
            shards * per_row, LAT
        )
        width = steps * ROPE
        part = packed[:, r * width : (r + 1) * width]
        turned = part * cos_ref[r : r + 1] + swap_halves(part) * sin_ref[r : r + 1]
        turned = jnp.stack(
            [
                turned[:, s * ROPE : (s + 1) * ROPE].reshape(shards, heads, ROPE)
                for s in range(steps)
            ],
            axis=1,
        ).reshape(shards * per_row, ROPE)
        q_scr[r, :, LAT:] = turned.astype(BF16)
        copies[r].wait()
        scores = jnp.dot(q_scr[r], keys_ref[r], preferred_element_type=F32)
        slot = lax.broadcasted_iota(jnp.int32, scores.shape, 1)
        scored.append(jnp.where(slot < live, scores, FLOOR))
    lse_rows = []
    for r in range(rows):
        scores = scored[r]
        top = jnp.max(scores, axis=1, keepdims=True)
        weights = jnp.exp2((scores - top) * (SCALE * LOG2E))
        total = jnp.sum(weights, axis=1, keepdims=True)
        mixed = lax.dot_general(
            weights.astype(BF16), keys_ref[r, :LAT, :], NT, preferred_element_type=F32
        )
        mixed = (mixed * (1.0 / total)).astype(BF16).reshape(shards, per_row, LAT)
        for lanes in range(LAT // 128):
            first = lanes * count + r * per_row
            out_ref[:, first : first + per_row, :] = mixed[:, :, lanes * 128 : (lanes + 1) * 128]
        lse = jnp.where(lengths_ref[r] > first_slot, top * SCALE + jnp.log(total), FLOOR)
        lse_rows.append(as_rows(lse.reshape(shards, per_row, 1)))
    tail = jnp.zeros((shards, heads, 128), F32)
    which = lax.broadcasted_iota(jnp.int32, tail.shape, 1)
    for r in range(rows):
        rest = lse_rows[r]
        for term in range(3):
            piece = rest.astype(BF16).astype(F32)
            tail = jnp.where(which == 3 * r + term, piece[:, None, :], tail)
            rest = rest - piece
    out_ref[:, LAT // 128 * count :, :] = tail.astype(BF16)


def attend(lengths, gathered, cos, sin, keys):
    rows, width, span = keys.shape
    shards, stride, _ = gathered.shape
    per_row = (stride - 8) // rows
    return pl.pallas_call(
        attend_kernel,
        out_shape=jax.ShapeDtypeStruct((shards, (stride - 8) * LAT // 128 + 8, 128), BF16),
        in_specs=[smem()] + [vmem()] * 3 + [pl.BlockSpec(memory_space=pltpu.HBM)],
        out_specs=vmem(),
        scratch_shapes=[
            pltpu.VMEM(keys.shape, BF16),
            pltpu.VMEM((rows, shards * per_row, width), BF16),
            pltpu.SemaphoreType.DMA((rows,)),
        ],
        compiler_params=pltpu.CompilerParams(vmem_limit_bytes=50 * 1024 * 1024),
        cost_estimate=pl.CostEstimate(
            flops=2 * rows * shards * per_row * span * (width + LAT),
            bytes_accessed=keys.size * 2 + gathered.size * 4,
            transcendentals=rows * shards * per_row * span,
        ),
        name="attend",
    )(lengths, gathered, cos, sin, keys)


def merge_kernel(offsets, got_ref, fresh_ref, fresh_lse_ref, *refs):
    *up_refs, out_ref, up = refs
    steps, rows, heads, _ = out_ref.shape
    shards = got_ref.shape[0]
    count = steps * rows * heads
    per_row = count // rows
    line = lax.axis_index("dp")
    chips = lax.axis_size("dp") // 2
    z = line // 2
    own = 1 - 2 * (line % 2)
    for ref, mine, spans in zip(up_refs, (1, 1, 1, -1, -1), offsets):
        depth = ref.shape[2]
        for b, offset in enumerate(spans):
            chip = (z + own * (mine * offset) + chips) % chips
            up[:, pl.ds(pl.multiple_of(chip * depth, depth), depth), :] = ref[b]
    tail = got_ref[:, LAT // 128 * count :, :].astype(F32)
    sub = lax.broadcasted_iota(jnp.int32, (per_row, 128), 0)
    lane = lax.broadcasted_iota(jnp.int32, (per_row, 128), 1)
    eye = sub == lane

    def column(row):
        return jnp.sum(jnp.where(eye, row, 0.0), axis=1, keepdims=True)

    merged = []
    for r in range(rows):
        spread = tail[:, 3 * r] + tail[:, 3 * r + 1] + tail[:, 3 * r + 2]
        own = fresh_lse_ref[r : r + 1]
        top = jnp.maximum(jnp.max(spread, axis=0, keepdims=True), own)
        factor = jnp.exp(spread - top)
        own_factor = jnp.exp(own - top)
        scale = 1.0 / (jnp.sum(factor, axis=0, keepdims=True) + own_factor)
        factor = factor * scale
        first = r * per_row
        total = column(own_factor * scale) * fresh_ref[first : first + per_row]
        for d in range(shards):
            piece = jnp.concatenate(
                [
                    got_ref[d, lanes * count + first : lanes * count + first + per_row, :]
                    for lanes in range(LAT // 128)
                ],
                axis=1,
            ).astype(F32)
            total += column(factor[d : d + 1]) * piece
        merged.append(total)
    latent = jnp.concatenate(merged, axis=0).astype(BF16)
    head = lax.broadcasted_iota(jnp.int32, (count, 128), 0) % heads
    result = jnp.zeros((count, 128), F32)
    for h in range(heads):
        product = jnp.dot(latent, up[h], preferred_element_type=F32)
        result = jnp.where(head == h, product, result)
    for r in range(rows):
        for s in range(steps):
            first = (r * steps + s) * heads
            out_ref[s, r] = result[first : first + heads]


def merge(got, fresh, fresh_lse, ups, offsets, steps, rows):
    _, heads, depth, width = ups[0].shape
    return pl.pallas_call(
        functools.partial(merge_kernel, offsets),
        out_shape=jax.ShapeDtypeStruct((steps, rows, heads, width), F32),
        in_specs=[vmem()] * (3 + len(ups)),
        out_specs=vmem(),
        scratch_shapes=[pltpu.VMEM((heads, LAT, width), BF16)],
        compiler_params=pltpu.CompilerParams(vmem_limit_bytes=16 * 1024 * 1024),
        name="merge",
    )(got, fresh, fresh_lse, *ups)


def body(queries, latent_cache, new_latent, lengths, value_up):
    steps, rows, heads, _ = queries.shape
    shards = lax.axis_size("ctx")
    lines = lax.axis_size("dp")
    chips = lines // 2

    def from_line(x, reach):
        pairs = []
        for line in range(lines):
            z, core = line // 2, line % 2
            sign = 1 - 2 * core
            pairs.append((((z + sign * reach) % chips) * 2 + core, line))
        return lax.ppermute(x, "dp", pairs)

    def from_core(x):
        return lax.ppermute(x, "dp", [(i, i ^ 1) for i in range(lines)])

    pair_index = jnp.arange(HALF, dtype=F32)
    frequency = jnp.power(F32(10000.0), -2.0 * pair_index / ROPE)
    positions = (lengths[:, None] + jnp.arange(steps, dtype=jnp.int32)[None, :]).astype(F32)
    angles = positions[..., None] * frequency
    packed = pack_queries(queries, shards)
    packed, value_up = lax.optimization_barrier((packed, value_up))
    gathered = lax.all_to_all(packed, "ctx", 0, 0, tiled=True)

    fresh, fresh_lse, cos, sin, near = fresh_part(
        queries, new_latent, jnp.cos(angles), jnp.sin(angles), value_up
    )
    near = lax.all_gather(
        near, "dp", axis=1, tiled=True, axis_index_groups=[[2 * z, 2 * z + 1] for z in range(chips)]
    )[None]
    held = jnp.concatenate([near, from_line(near, 4)], axis=0)
    second = from_line(held, 2)
    partial = attend(lengths, gathered, cos, sin, jnp.swapaxes(latent_cache, 1, 2))
    partial, second = lax.optimization_barrier((partial, second))
    got = lax.all_to_all(partial, "ctx", 0, 0, tiled=True)
    held = jnp.concatenate([held, second], axis=0)
    third = from_line(held, 1)
    eighth = from_line(third[-1:], 1)
    ups = (held, third, eighth, from_core(held), from_core(third))
    even, odd = (0, 4, 2, 6), (1, 5, 3, 7)
    return merge(got, fresh, fresh_lse, ups, (even, odd, (8,), even, odd), steps, rows)


def solution(mesh):
    placed = (
        P(None, "dp", "ctx", None),
        P("dp", "ctx", None),
        P(None, "dp", None),
        P("dp"),
        P("ctx", "dp", None),
    )
    return jax.shard_map(
        body, mesh=mesh, in_specs=placed, out_specs=P(None, "dp", "ctx", None), check_vma=False
    )
```

time: 84.9 us -> 74.2 us (0.87)
  starting transfers between devices: 52.4 us -> 42.8 us
  local copies, waits for them, and re-layouts: 9.99 us -> 1.35 us
  blocking collectives: 0 us -> 4.92 us
  waiting for transfers between devices: 5.98 us -> 9.74 us
    ppermute x4, starting transfers between devices: 29.2 us -> 16.6 us  [from_line(): return lax.ppermute(x, 'dp', pairs)]
    unnamed x15 -> x10, local copies, waits for them, and re-layouts: 9.71 us -> 1.35 us
    all_gather x0 -> x1, blocking collectives: none -> 4.92 us  [body(): lax.all_gather(near, 'dp', axis=1, tiled=True, axis_index_groups=[[2 * z,...]
    ppermute x4, waiting for transfers between devices: 5.97 us -> 9.73 us  [from_line(): return lax.ppermute(x, 'dp', pairs)]
    ppermute x1 -> x2, starting transfers between devices: 8.83 us -> 11.6 us  [from_core(): return lax.ppermute(x, 'dp', [(i, i ^ 1) for i in range(lines)])]
  transfers between devices with their start and end apart: 7 -> 8, of which waited for: 2 -> 2; matrix products, arithmetic and copies ran while one was open for 9% -> 1% of each run, Pallas kernels for 12% -> 14%
where the time goes in v2:
time: 74.2 us; the launch traced here: 73.6 us
  starting transfers between devices  42.8 us (58%)
  Pallas kernels  13.8 us (19%)
  waiting for transfers between devices  9.74 us (13%)
  blocking collectives  4.92 us (7%)
  local copies, waits for them, and re-layouts  1.35 us (2%)
  other arithmetic  0.84 us (1%)
    ppermute x4, starting transfers between devices, from_line(): return lax.ppermute(x, 'dp', pairs)  16.6 us
    ppermute x2, starting transfers between devices, from_core(): return lax.ppermute(x, 'dp', [(i, i ^ 1) for i in range(lines)])  11.6 us
    ppermute x4, waiting for transfers between devices, from_line(): return lax.ppermute(x, 'dp', pairs)  9.73 us
    pallas_call x1, Pallas kernels, attend(): pl.pallas_call(attend_kernel, out_shape=jax.ShapeDtypeStruct((shards, (st...  8.46 us
    all_to_all x1, starting transfers between devices, body(): gathered = lax.all_to_all(packed, 'ctx', 0, 0, tiled=True)  7.72 us
    all_to_all x1, starting transfers between devices, body(): got = lax.all_to_all(partial, 'ctx', 0, 0, tiled=True)  6.88 us
    all_gather x1, blocking collectives, body(): lax.all_gather(near, 'dp', axis=1, tiled=True, axis_index_groups=[[2 * z,...  4.92 us
    pallas_call x1, Pallas kernels, fresh_part(): pl.pallas_call(fresh_kernel, out_shape=(jax.ShapeDtypeStruct((count, LAT)...  2.1 us
  transfers between devices with their start and end apart: 8, of which 2 were waited for; matrix products, arithmetic and copies ran while one was open for 1% of the time, Pallas kernels for 14%

profile of v2, /device:TPU:1, one launch (start us, length us, event | category | flops | bytes accessed | tf_op | source)
XLA Modules:
  0.0 73.6 jit_solution(16169361765254066982)
XLA Ops:
  0.0 2.0 %pack_queries.1 = bf16[16,72,512]{2,1,0:T(8,128)(2,1)} custom-call(bf16[4,2,8,576]{3,2,1,0:T(8,128)(2,1)} %q_ref.3), custom_call_target="tpu_custom_call" | custom-call | tf_op jit(solution)/shard_map/pack_queries/pallas_call | solution.py:56
  2.0 7.7 %all-to-all-start = ((bf16[16,72,512]{2,1,0:T(8,128)(2,1)}), bf16[16,72,512]{2,1,0:T(8,128)(2,1)S(1)}, u32[]{:S(2)}, u32[]{:S(2)}) async-start(bf16[16,72,512]{2,1,0:T(8,128)(2,1)} %pack_queries.1), calls=%async_computation | async-start | bytes 2359296 | tf_op jit(solution)/shard_map/all_to_all | solution.py:317
  9.7 0.1 add_convert_fusion
  9.8 0.7 multiply_sine_fusion
  10.5 2.1 %fresh_part.1 = (f32[64,512]{1,0:T(8,128)}, f32[2,128]{1,0:T(2,128)}, f32[2,256]{1,0:T(2,128)}, f32[2,256]{1,0:T(2,128)}, bf16[8,16,128]{2,1,0:T(8,128)(2,1)}) custom-call(bf16[4,2,8,576]{3,2,1,0:T(8,128)(2,1)} %q_ref.3, bf16[4,2,576]{2,1,0:T(2,128)(2,1)} %new_ref.1, f32[2,4,32]{2,1,0:T(4,128)} %get-tuple-element.24.cos_ref, ...), custom_call_target="tpu_custom_call" | custom-call | flops 99999997952 | tf_op jit(solution)/shard_map/fresh_part/pallas_call | solution.py:124
  12.6 4.9 %all_gather.3 = bf16[8,32,128]{2,1,0:T(8,128)(2,1)S(1)} all-gather(bf16[8,16,128]{2,1,0:T(8,128)(2,1)} %get-tuple-element.18), channel_id=1, replica_groups={{0,16},{32,48},{64,80},{96,112},{128,144},{160,176},{192,208},{224,240}..., dimensions={1}, use_global_device_ids=true | all-gather | bytes 98304 | tf_op jit(solution)/shard_map/all_gather | solution.py:322
  17.6 6.8 %collective-permute-start = (bf16[1,8,32,128]{3,2,1,0:T(8,128)(2,1)S(1)}, bf16[1,8,32,128]{3,2,1,0:T(8,128)(2,1)S(1)}, u32[]{:S(2)}, u32[]{:S(2)}) collective-permute-start(bf16[1,8,32,128]{3,2,1,0:T(8,128)(2,1)S(1)} %bitcast.2), channel_id=1, source_target_pairs={{128,0},{400,16},{160,32},{432,48},{192,64},{464,80},{224,96},{496... | collective-permute-start | bytes 196616 | tf_op jit(solution)/shard_map/ppermute | solution.py:306
  24.3 5.6 %collective-permute-done = bf16[1,8,32,128]{3,2,1,0:T(8,128)(2,1)S(1)} collective-permute-done((bf16[1,8,32,128]{3,2,1,0:T(8,128)(2,1)S(1)}, bf16[1,8,32,128]{3,2,1,0:T(8,128)(2,1)S(1)}, u32[]{:S(2)}, u32[]{:S(2)}) %collective-permute-start) | collective-permute-done | bytes 65568 | tf_op jit(solution)/shard_map/ppermute | solution.py:306
  29.9 4.5 %collective-permute-start.1 = (bf16[2,8,32,128]{3,2,1,0:T(8,128)(2,1)S(1)}, bf16[2,8,32,128]{3,2,1,0:T(8,128)(2,1)S(1)}, u32[]{:S(2)}, u32[]{:S(2)}) collective-permute-start(bf16[2,8,32,128]{3,2,1,0:T(8,128)(2,1)S(1)} %pad_maximum_fusion.1), channel_id=1, source_target_pairs={{64,0},{464,16},{96,32},{496,48},{128,64},{16,80},{160,96},{48,112... | collective-permute-start | bytes 393224 | tf_op jit(solution)/shard_map/ppermute | solution.py:306
  34.4 0.0 all-to-all-done.q_ref
  34.5 0.7 copy-done.3
  35.1 0.7 copy-done.4
  35.8 8.5 %attend.1 = bf16[16,264,128]{2,1,0:T(8,128)(2,1)} custom-call(s32[2]{0:T(128)S(1)} %copy-done.2, bf16[16,72,512]{2,1,0:T(8,128)(2,1)S(1)} %all-to-all-done.q_ref, f32[2,256]{1,0:T(2,128)S(1)} %copy-done.3, f32[2,256]{1,0:T(2,128)S(1)} %copy-done.4, bf16[2,576,1536]{2,1,0:T(8,128)(2,1)} %bitcast.5), custom_call_target="tpu_custom_call" | custom-call | flops 3422552064 | bytes 5898240 | tf_op jit(solution)/shard_map/attend/pallas_call | solution.py:205
  44.3 0.0 collective-permute-done.1
  44.3 6.9 %all-to-all-start.1 = ((bf16[16,264,128]{2,1,0:T(8,128)(2,1)}), bf16[16,264,128]{2,1,0:T(8,128)(2,1)S(1)}, u32[]{:S(2)}, u32[]{:S(2)}) async-start(bf16[16,264,128]{2,1,0:T(8,128)(2,1)} %attend.1), calls=%async_computation.1 | async-start | bytes 2162688 | tf_op jit(solution)/shard_map/all_to_all | solution.py:329
  51.2 3.2 %collective-permute-start.2 = (bf16[4,8,32,128]{3,2,1,0:T(8,128)(2,1)S(1)}, bf16[4,8,32,128]{3,2,1,0:T(8,128)(2,1)S(1)}, u32[]{:S(2)}, u32[]{:S(2)}) collective-permute-start(bf16[4,8,32,128]{3,2,1,0:T(8,128)(2,1)S(1)} %pad_maximum_fusion.refs_0_), channel_id=1, source_target_pairs={{32,0},{496,16},{64,32},{16,48},{96,64},{48,80},{128,96},{80,112},... | collective-permute-start | bytes 786440 | tf_op jit(solution)/shard_map/ppermute | solution.py:306
  54.5 6.9 %collective-permute-start.4 = (bf16[4,8,32,128]{3,2,1,0:T(8,128)(2,1)S(1)}, bf16[4,8,32,128]{3,2,1,0:T(8,128)(2,1)S(1)}, u32[]{:S(2)}, u32[]{:S(2)}) collective-permute-start(bf16[4,8,32,128]{3,2,1,0:T(8,128)(2,1)S(1)} %pad_maximum_fusion.refs_0_), channel_id=1, source_target_pairs={{0,16},{16,0},{32,48},{48,32},{64,80},{80,64},{96,112},{112,96},{1... | collective-permute-start | bytes 786440 | tf_op jit(solution)/shard_map/ppermute | solution.py:309
  61.4 0.0 collective-permute-done.2.refs_1_
  61.4 4.7 %collective-permute-start.5 = (bf16[4,8,32,128]{3,2,1,0:T(8,128)(2,1)S(1)}, bf16[4,8,32,128]{3,2,1,0:T(8,128)(2,1)S(1)}, u32[]{:S(2)}, u32[]{:S(2)}) collective-permute-start(bf16[4,8,32,128]{3,2,1,0:T(8,128)(2,1)S(1)} %collective-permute-done.2.refs_1_), channel_id=1, source_target_pairs={{0,16},{16,0},{32,48},{48,32},{64,80},{80,64},{96,112},{112,96},{1... | collective-permute-start | bytes 786440 | tf_op jit(solution)/shard_map/ppermute | solution.py:309
  66.1 2.1 %collective-permute-start.3 = (bf16[1,8,32,128]{3,2,1,0:T(8,128)(2,1)S(1)}, bf16[1,8,32,128]{3,2,1,0:T(8,128)(2,1)S(1)}, u32[]{:S(2)}, u32[]{:S(2)}) collective-permute-start(bf16[1,8,32,128]{3,2,1,0:T(8,128)(2,1)S(1)} %slice.4), channel_id=1, source_target_pairs={{32,0},{496,16},{64,32},{16,48},{96,64},{48,80},{128,96},{80,112},... | collective-permute-start | bytes 196616 | tf_op jit(solution)/shard_map/ppermute | solution.py:306
  68.2 0.0 collective-permute-done.4.refs_3_
  68.2 4.1 %collective-permute-done.3.refs_2_ = bf16[1,8,32,128]{3,2,1,0:T(8,128)(2,1)S(1)} collective-permute-done((bf16[1,8,32,128]{3,2,1,0:T(8,128)(2,1)S(1)}, bf16[1,8,32,128]{3,2,1,0:T(8,128)(2,1)S(1)}, u32[]{:S(2)}, u32[]{:S(2)}) %collective-permute-start.3) | collective-permute-done | bytes 65568 | tf_op jit(solution)/shard_map/ppermute | solution.py:306
  72.3 0.0 collective-permute-done.5.refs_4_
  72.4 1.2 %merge.1 = f32[4,2,8,128]{3,2,1,0:T(8,128)} custom-call(bf16[16,264,128]{2,1,0:T(8,128)(2,1)S(1)} %all-to-all-done.1.got_ref, f32[64,512]{1,0:T(8,128)S(1)} %copy-done, f32[2,128]{1,0:T(2,128)S(1)} %copy-done.1, bf16[4,8,32,128]{3,2,1,0:T(8,128)(2,1)S(1)} %pad_maximum_fusion.refs_0_, bf16[4,8,32,128]{3,2,1,0:T(8,128)(2,1)S(1)} %collective-permute-done.2.refs_1_, ...), custom_call_target="tpu_custom_call" | custom-call | tf_op jit(solution)/shard_map/merge/pallas_call | solution.py:283
  (13 shorter events, 0.1 us)
Async XLA Ops:
  2.0 7.7 %copy-start.2 = (s32[2]{0:T(128)S(1)}, s32[2]{0:T(128)}, u32[]{:S(2)}) copy-start(s32[2]{0:T(128)} %lengths_ref.1) | copy-start | bytes 28
  2.0 32.4 %all-to-all-start = ((bf16[16,72,512]{2,1,0:T(8,128)(2,1)}), bf16[16,72,512]{2,1,0:T(8,128)(2,1)S(1)}, u32[]{:S(2)}, u32[]{:S(2)}) async-start(bf16[16,72,512]{2,1,0:T(8,128)(2,1)} %pack_queries.1), calls=%async_computation | async-start | bytes 2359296 | tf_op jit(solution)/shard_map/all_to_all | solution.py:317
  17.6 12.4 %collective-permute-start = (bf16[1,8,32,128]{3,2,1,0:T(8,128)(2,1)S(1)}, bf16[1,8,32,128]{3,2,1,0:T(8,128)(2,1)S(1)}, u32[]{:S(2)}, u32[]{:S(2)}) collective-permute-start(bf16[1,8,32,128]{3,2,1,0:T(8,128)(2,1)S(1)} %bitcast.2), channel_id=1, source_target_pairs={{128,0},{400,16},{160,32},{432,48},{192,64},{464,80},{224,96},{496... | collective-permute-start | bytes 196616 | tf_op jit(solution)/shard_map/ppermute | solution.py:306
  29.9 14.3 %collective-permute-start.1 = (bf16[2,8,32,128]{3,2,1,0:T(8,128)(2,1)S(1)}, bf16[2,8,32,128]{3,2,1,0:T(8,128)(2,1)S(1)}, u32[]{:S(2)}, u32[]{:S(2)}) collective-permute-start(bf16[2,8,32,128]{3,2,1,0:T(8,128)(2,1)S(1)} %pad_maximum_fusion.1), channel_id=1, source_target_pairs={{64,0},{464,16},{96,32},{496,48},{128,64},{16,80},{160,96},{48,112... | collective-permute-start | bytes 393224 | tf_op jit(solution)/shard_map/ppermute | solution.py:306
  34.4 0.7 copy-start.3
  35.1 0.7 copy-start.4
  44.3 28.1 %copy-start = (f32[64,512]{1,0:T(8,128)S(1)}, f32[64,512]{1,0:T(8,128)}, u32[]{:S(2)}) copy-start(f32[64,512]{1,0:T(8,128)} %get-tuple-element.20.fresh_ref) | copy-start | bytes 393220
  44.3 28.1 %copy-start.1 = (f32[2,128]{1,0:T(2,128)S(1)}, f32[2,128]{1,0:T(2,128)}, u32[]{:S(2)}) copy-start(f32[2,128]{1,0:T(2,128)} %get-tuple-element.21.fresh_lse_ref) | copy-start | bytes 3076
  44.3 28.1 %all-to-all-start.1 = ((bf16[16,264,128]{2,1,0:T(8,128)(2,1)}), bf16[16,264,128]{2,1,0:T(8,128)(2,1)S(1)}, u32[]{:S(2)}, u32[]{:S(2)}) async-start(bf16[16,264,128]{2,1,0:T(8,128)(2,1)} %attend.1), calls=%async_computation.1 | async-start | bytes 2162688 | tf_op jit(solution)/shard_map/all_to_all | solution.py:329
  51.2 10.2 %collective-permute-start.2 = (bf16[4,8,32,128]{3,2,1,0:T(8,128)(2,1)S(1)}, bf16[4,8,32,128]{3,2,1,0:T(8,128)(2,1)S(1)}, u32[]{:S(2)}, u32[]{:S(2)}) collective-permute-start(bf16[4,8,32,128]{3,2,1,0:T(8,128)(2,1)S(1)} %pad_maximum_fusion.refs_0_), channel_id=1, source_target_pairs={{32,0},{496,16},{64,32},{16,48},{96,64},{48,80},{128,96},{80,112},... | collective-permute-start | bytes 786440 | tf_op jit(solution)/shard_map/ppermute | solution.py:306
  54.5 13.7 %collective-permute-start.4 = (bf16[4,8,32,128]{3,2,1,0:T(8,128)(2,1)S(1)}, bf16[4,8,32,128]{3,2,1,0:T(8,128)(2,1)S(1)}, u32[]{:S(2)}, u32[]{:S(2)}) collective-permute-start(bf16[4,8,32,128]{3,2,1,0:T(8,128)(2,1)S(1)} %pad_maximum_fusion.refs_0_), channel_id=1, source_target_pairs={{0,16},{16,0},{32,48},{48,32},{64,80},{80,64},{96,112},{112,96},{1... | collective-permute-start | bytes 786440 | tf_op jit(solution)/shard_map/ppermute | solution.py:309
  61.4 11.0 %collective-permute-start.5 = (bf16[4,8,32,128]{3,2,1,0:T(8,128)(2,1)S(1)}, bf16[4,8,32,128]{3,2,1,0:T(8,128)(2,1)S(1)}, u32[]{:S(2)}, u32[]{:S(2)}) collective-permute-start(bf16[4,8,32,128]{3,2,1,0:T(8,128)(2,1)S(1)} %collective-permute-done.2.refs_1_), channel_id=1, source_target_pairs={{0,16},{16,0},{32,48},{48,32},{64,80},{80,64},{96,112},{112,96},{1... | collective-permute-start | bytes 786440 | tf_op jit(solution)/shard_map/ppermute | solution.py:309
  66.1 6.2 %collective-permute-start.3 = (bf16[1,8,32,128]{3,2,1,0:T(8,128)(2,1)S(1)}, bf16[1,8,32,128]{3,2,1,0:T(8,128)(2,1)S(1)}, u32[]{:S(2)}, u32[]{:S(2)}) collective-permute-start(bf16[1,8,32,128]{3,2,1,0:T(8,128)(2,1)S(1)} %slice.4), channel_id=1, source_target_pairs={{32,0},{496,16},{64,32},{16,48},{96,64},{48,80},{128,96},{80,112},... | collective-permute-start | bytes 196616 | tf_op jit(solution)/shard_map/ppermute | solution.py:306

commit v3 on v2

--- a/solution.py
+++ b/solution.py
@@ -2,6 +2,7 @@
 
 import jax
 import jax.numpy as jnp
+import numpy as np
 from jax import lax
 from jax.experimental import pallas as pl
 from jax.experimental.pallas import tpu as pltpu
@@ -62,25 +63,38 @@
     )(queries)
 
 
-def fresh_kernel(
-    q_ref, new_ref, cos_ref, sin_ref, up_ref, mixed_ref, lse_ref, wide_cos_ref, wide_sin_ref, near_ref
-):
+def rotation(lengths_ref, steps, shape, step_of, row_of):
+    row = lax.broadcasted_iota(jnp.int32, shape, 0)
+    lane = lax.broadcasted_iota(jnp.int32, shape, 1)
+    which = row_of(row)
+    position = jnp.zeros(shape, jnp.int32)
+    for r in range(lengths_ref.shape[0]):
+        position = jnp.where(which == r, lengths_ref[r], position)
+    position += step_of(row, lane)
+    frequency = jnp.zeros(shape, F32)
+    for i in range(HALF):
+        value = float(np.float32(10000.0 ** (-2.0 * i / ROPE)))
+        frequency = jnp.where(lane % HALF == i, value, frequency)
+    angle = position.astype(F32) * frequency
+    sine = jnp.sin(angle)
+    return jnp.cos(angle), jnp.where(lane % ROPE < HALF, -sine, sine)
+
+
+def fresh_kernel(lengths_ref, q_ref, new_ref, mixed_ref, lse_ref):
     steps, rows, heads, _ = q_ref.shape
     count = rows * steps * heads
     keys = rows * steps
-    near_ref[...] = up_ref[...]
+    cos, sin = rotation(
+        lengths_ref, steps, (keys, 2 * ROPE), lambda row, _: row % steps, lambda row: row // steps
+    )
     q_lat = []
     q_rot = []
     key_lat = []
     key_rot = []
     for r in range(rows):
         for s in range(steps):
-            cos = cos_ref[r, s : s + 1]
-            sin = sin_ref[r, s : s + 1]
-            row_cos = jnp.concatenate([cos, cos, cos, cos], axis=1)
-            row_sin = jnp.concatenate([-sin, sin, -sin, sin], axis=1)
-            wide_cos_ref[r : r + 1, s * ROPE : (s + 1) * ROPE] = row_cos[:, :ROPE]
-            wide_sin_ref[r : r + 1, s * ROPE : (s + 1) * ROPE] = row_sin[:, :ROPE]
+            row_cos = cos[r * steps + s : r * steps + s + 1]
+            row_sin = sin[r * steps + s : r * steps + s + 1]
             block = q_ref[s, r].astype(F32)
             q_lat.append(block[:, :LAT])
             wide = jnp.concatenate([block[:, LAT:], block[:, LAT:]], axis=1)
@@ -118,7 +132,7 @@
     return jnp.sum(jnp.where(row == lane, column, 0.0), axis=1)
 
 
-def fresh_part(queries, new_latent, cos, sin, value_up):
+def fresh_part(lengths, queries, new_latent):
     steps, rows, heads, _ = queries.shape
     count = steps * rows * heads
     return pl.pallas_call(
@@ -126,67 +140,129 @@
         out_shape=(
             jax.ShapeDtypeStruct((count, LAT), F32),
             jax.ShapeDtypeStruct((rows, 128), F32),
-            jax.ShapeDtypeStruct((rows, steps * ROPE), F32),
-            jax.ShapeDtypeStruct((rows, steps * ROPE), F32),
-            jax.ShapeDtypeStruct(value_up.shape, BF16),
         ),
-        in_specs=[vmem()] * 5,
-        out_specs=(vmem(),) * 5,
-        cost_estimate=pl.CostEstimate(flops=10**11, bytes_accessed=0, transcendentals=0),
+        in_specs=[smem()] + [vmem()] * 2,
+        out_specs=(vmem(),) * 2,
         name="fresh_part",
-    )(queries, new_latent, cos, sin, value_up)
-
-
-def attend_kernel(lengths_ref, q_ref, cos_ref, sin_ref, cache_ref, out_ref, keys_ref, q_scr, sems):
-    rows, _, span = cache_ref.shape
+    )(lengths, queries, new_latent)
+
+
+CHUNK = 512
+PARTS = 2
+
+
+def attend_kernel(lengths_ref, q_ref, cache_ref, out_hbm, *scratch):
+    keys_ref, q_scr, s_scr, p_scr, out_ref, sems, out_sems = scratch
+    rows, width, span = cache_ref.shape
     shards, stride, _ = q_ref.shape
     heads = 8
     count = stride - heads
-    copies = [
-        pltpu.make_async_copy(cache_ref.at[r], keys_ref.at[r], sems.at[r]) for r in range(rows)
-    ]
-    for copy in copies:
-        copy.start()
     per_row = count // rows
     steps = per_row // heads
+    many = shards * per_row
+    deep = width // PARTS
+    copies = [
+        [
+            pltpu.make_async_copy(
+                cache_ref.at[r, pl.ds(part * deep, deep)],
+                keys_ref.at[r, pl.ds(part * deep, deep)],
+                sems.at[r, part],
+            )
+            for part in range(PARTS)
+        ]
+        for r in range(rows)
+    ]
+    for copy in copies[0]:
+        copy.start()
     packed = q_ref[:, count:, :].astype(F32).reshape(shards * heads, LAT)
     first_slot = lax.axis_index("ctx") * span
-    scored = []
+    pad = keys_ref.shape[1] - width
+    cos, sin = rotation(
+        lengths_ref, steps, (8, steps * ROPE), lambda _, lane: lane // ROPE, lambda row: row
+    )
     for r in range(rows):
         live = lengths_ref[r] - first_slot
-        q_scr[r, :, :LAT] = q_ref[:, r * per_row : (r + 1) * per_row, :].reshape(
-            shards * per_row, LAT
-        )
-        width = steps * ROPE
-        part = packed[:, r * width : (r + 1) * width]
-        turned = part * cos_ref[r : r + 1] + swap_halves(part) * sin_ref[r : r + 1]
+        slot = lax.broadcasted_iota(jnp.int32, (pad, span), 1)
+        line = lax.broadcasted_iota(jnp.int32, (pad, span), 0)
+        keys_ref[r, width:, :] = jnp.where((line == 0) & (slot >= live), FLOOR, 0.0).astype(BF16)
+        q_scr[r, :, :LAT] = q_ref[:, r * per_row : (r + 1) * per_row, :].reshape(many, LAT)
+        part = packed[:, r * steps * ROPE : (r + 1) * steps * ROPE]
+        turned = part * cos[r : r + 1] + swap_halves(part) * sin[r : r + 1]
         turned = jnp.stack(
             [
                 turned[:, s * ROPE : (s + 1) * ROPE].reshape(shards, heads, ROPE)
                 for s in range(steps)
             ],
             axis=1,
-        ).reshape(shards * per_row, ROPE)
-        q_scr[r, :, LAT:] = turned.astype(BF16)
-        copies[r].wait()
-        scores = jnp.dot(q_scr[r], keys_ref[r], preferred_element_type=F32)
-        slot = lax.broadcasted_iota(jnp.int32, scores.shape, 1)
-        scored.append(jnp.where(slot < live, scores, FLOOR))
-    lse_rows = []
-    for r in range(rows):
-        scores = scored[r]
-        top = jnp.max(scores, axis=1, keepdims=True)
-        weights = jnp.exp2((scores - top) * (SCALE * LOG2E))
-        total = jnp.sum(weights, axis=1, keepdims=True)
-        mixed = lax.dot_general(
-            weights.astype(BF16), keys_ref[r, :LAT, :], NT, preferred_element_type=F32
+        ).reshape(many, ROPE)
+        lane = lax.broadcasted_iota(jnp.int32, (many, pad), 1)
+        one = jnp.where(lane == 0, 1.0, 0.0)
+        q_scr[r, :, LAT:] = jnp.concatenate([turned, one], axis=1).astype(BF16)
+
+    half = LAT // 128 * per_row
+    outs = [
+        pltpu.make_async_copy(out_ref.at[:, pl.ds(0, half)], out_hbm.at[:, pl.ds(0, half)], out_sems.at[0]),
+        pltpu.make_async_copy(
+            out_ref.at[:, pl.ds(half, out_hbm.shape[1] - half)],
+            out_hbm.at[:, pl.ds(half, out_hbm.shape[1] - half)],
+            out_sems.at[1],
+        ),
+    ]
+
+    def score(r, first, top):
+        part = jnp.dot(
+            q_scr[r], keys_ref[r, :, first : first + CHUNK], preferred_element_type=F32
         )
+        s_scr[r, :, first : first + CHUNK] = part
+        for lanes in range(0, CHUNK, 128):
+            block = part[:, lanes : lanes + 128]
+            top = block if top is None else jnp.maximum(top, block)
+        return top
+
+    def weigh(r, first, level, total):
+        part = jnp.exp2((s_scr[r, :, first : first + CHUNK] - level) * (SCALE * LOG2E))
+        p_scr[r, :, first : first + CHUNK] = part.astype(BF16)
+        for lanes in range(0, CHUNK, 128):
+            block = part[:, lanes : lanes + 128]
+            total = block if total is None else total + block
+        return total
+
+    def mix(r):
+        return lax.dot_general(p_scr[r], keys_ref[r, :LAT, :], NT, preferred_element_type=F32)
+
+    def finish(r, level, total, mixed):
+        total = jnp.sum(total, axis=1, keepdims=True)
         mixed = (mixed * (1.0 / total)).astype(BF16).reshape(shards, per_row, LAT)
         for lanes in range(LAT // 128):
-            first = lanes * count + r * per_row
+            first = (r * (LAT // 128) + lanes) * per_row
             out_ref[:, first : first + per_row, :] = mixed[:, :, lanes * 128 : (lanes + 1) * 128]
-        lse = jnp.where(lengths_ref[r] > first_slot, top * SCALE + jnp.log(total), FLOOR)
-        lse_rows.append(as_rows(lse.reshape(shards, per_row, 1)))
+        if r == 0:
+            outs[0].start()
+        lse = jnp.where(lengths_ref[r] > first_slot, level * SCALE + jnp.log(total), FLOOR)
+        return as_rows(lse.reshape(shards, per_row, 1))
+
+    levels = []
+    totals = [None] * rows
+    for r in range(rows):
+        for copy in copies[r]:
+            copy.wait()
+        if r + 1 < rows:
+            for copy in copies[r + 1]:
+                copy.start()
+        top = None
+        for first in range(0, span, CHUNK):
+            top = score(r, first, top)
+        levels.append(jnp.max(top, axis=1, keepdims=True))
+        if r == 0:
+            for first in range(0, span, CHUNK):
+                totals[0] = weigh(0, first, levels[0], totals[0])
+    lse_rows = []
+    for r in range(rows):
+        mixed = mix(r)
+        if r == rows - 2:
+            for first in range(0, span, CHUNK):
+                totals[r + 1] = weigh(r + 1, first, levels[r + 1], totals[r + 1])
+        lse_rows.append(finish(r, levels[r], totals[r], mixed))
     tail = jnp.zeros((shards, heads, 128), F32)
     which = lax.broadcasted_iota(jnp.int32, tail.shape, 1)
     for r in range(rows):
@@ -196,30 +272,38 @@
             tail = jnp.where(which == 3 * r + term, piece[:, None, :], tail)
             rest = rest - piece
     out_ref[:, LAT // 128 * count :, :] = tail.astype(BF16)
-
-
-def attend(lengths, gathered, cos, sin, keys):
+    outs[1].start()
+    for out in outs:
+        out.wait()
+
+
+def attend(lengths, gathered, keys):
     rows, width, span = keys.shape
     shards, stride, _ = gathered.shape
-    per_row = (stride - 8) // rows
+    many = (stride - 8) // rows * shards
+    padded = width + 64
     return pl.pallas_call(
         attend_kernel,
         out_shape=jax.ShapeDtypeStruct((shards, (stride - 8) * LAT // 128 + 8, 128), BF16),
-        in_specs=[smem()] + [vmem()] * 3 + [pl.BlockSpec(memory_space=pltpu.HBM)],
-        out_specs=vmem(),
+        in_specs=[smem(), vmem(), pl.BlockSpec(memory_space=pltpu.HBM)],
+        out_specs=pl.BlockSpec(memory_space=pltpu.HBM),
         scratch_shapes=[
-            pltpu.VMEM(keys.shape, BF16),
-            pltpu.VMEM((rows, shards * per_row, width), BF16),
-            pltpu.SemaphoreType.DMA((rows,)),
+            pltpu.VMEM((rows, padded, span), BF16),
+            pltpu.VMEM((rows, many, padded), BF16),
+            pltpu.VMEM((rows, many, span), F32),
+            pltpu.VMEM((rows, many, span), BF16),
+            pltpu.VMEM((shards, (stride - 8) * LAT // 128 + 8, 128), BF16),
+            pltpu.SemaphoreType.DMA((rows, PARTS)),
+            pltpu.SemaphoreType.DMA((2,)),
         ],
         compiler_params=pltpu.CompilerParams(vmem_limit_bytes=50 * 1024 * 1024),
         cost_estimate=pl.CostEstimate(
-            flops=2 * rows * shards * per_row * span * (width + LAT),
+            flops=2 * rows * many * span * (width + LAT),
             bytes_accessed=keys.size * 2 + gathered.size * 4,
-            transcendentals=rows * shards * per_row * span,
+            transcendentals=rows * many * span,
         ),
         name="attend",
-    )(lengths, gathered, cos, sin, keys)
+    )(lengths, gathered, keys)
 
 
 def merge_kernel(offsets, got_ref, fresh_ref, fresh_lse_ref, *refs):
@@ -259,8 +343,8 @@
         for d in range(shards):
             piece = jnp.concatenate(
                 [
-                    got_ref[d, lanes * count + first : lanes * count + first + per_row, :]
-                    for lanes in range(LAT // 128)
+                    got_ref[d, lanes * per_row : (lanes + 1) * per_row, :]
+                    for lanes in range(r * (LAT // 128), (r + 1) * (LAT // 128))
                 ],
                 axis=1,
             ).astype(F32)
@@ -308,28 +392,27 @@
     def from_core(x):
         return lax.ppermute(x, "dp", [(i, i ^ 1) for i in range(lines)])
 
-    pair_index = jnp.arange(HALF, dtype=F32)
-    frequency = jnp.power(F32(10000.0), -2.0 * pair_index / ROPE)
-    positions = (lengths[:, None] + jnp.arange(steps, dtype=jnp.int32)[None, :]).astype(F32)
-    angles = positions[..., None] * frequency
     packed = pack_queries(queries, shards)
-    packed, value_up = lax.optimization_barrier((packed, value_up))
+    packed, value_up, lengths = lax.optimization_barrier((packed, value_up, lengths))
     gathered = lax.all_to_all(packed, "ctx", 0, 0, tiled=True)
 
-    fresh, fresh_lse, cos, sin, near = fresh_part(
-        queries, new_latent, jnp.cos(angles), jnp.sin(angles), value_up
-    )
     near = lax.all_gather(
-        near, "dp", axis=1, tiled=True, axis_index_groups=[[2 * z, 2 * z + 1] for z in range(chips)]
+        value_up, "dp", axis=1, tiled=True,
+        axis_index_groups=[[2 * z, 2 * z + 1] for z in range(chips)],
     )[None]
-    held = jnp.concatenate([near, from_line(near, 4)], axis=0)
+    first = from_line(near, 4)
+
+    fresh, fresh_lse = fresh_part(lengths, queries, new_latent)
+    held = jnp.concatenate([near, first], axis=0)
+    held, fresh, fresh_lse = lax.optimization_barrier((held, fresh, fresh_lse))
     second = from_line(held, 2)
-    partial = attend(lengths, gathered, cos, sin, jnp.swapaxes(latent_cache, 1, 2))
+    partial = attend(lengths, gathered, jnp.swapaxes(latent_cache, 1, 2))
     partial, second = lax.optimization_barrier((partial, second))
     got = lax.all_to_all(partial, "ctx", 0, 0, tiled=True)
     held = jnp.concatenate([held, second], axis=0)
     third = from_line(held, 1)
-    eighth = from_line(third[-1:], 1)
+    eighth = from_line(second[-1:], 2)
+    third, eighth = lax.optimization_barrier((third, eighth))
     ups = (held, third, eighth, from_core(held), from_core(third))
     even, odd = (0, 4, 2, 6), (1, 5, 3, 7)
     return merge(got, fresh, fresh_lse, ups, (even, odd, (8,), even, odd), steps, rows)

time: 74.2 us -> 67 us (0.903)
  waiting for transfers between devices: 9.74 us -> 4.63 us
  local copies, waits for them, and re-layouts: 1.35 us -> 0.05 us
  starting transfers between devices: 42.8 us -> 43.7 us
  other arithmetic: 0.84 us -> 0.01 us
    ppermute x4, waiting for transfers between devices: 9.73 us -> 3.5 us  [from_line(): return lax.ppermute(x, 'dp', pairs)]
    ppermute x4, starting transfers between devices: 16.6 us -> 18.1 us  [from_line(): return lax.ppermute(x, 'dp', pairs)]
    unnamed x10 -> x9, local copies, waits for them, and re-layouts: 1.35 us -> 0.03 us
    ppermute x2, waiting for transfers between devices: 0.01 us -> 1.13 us  [from_core(): return lax.ppermute(x, 'dp', [(i, i ^ 1) for i in range(lines)])]
    ppermute x2, starting transfers between devices: 11.6 us -> 10.8 us  [from_core(): return lax.ppermute(x, 'dp', [(i, i ^ 1) for i in range(lines)])]
  transfers between devices with their start and end apart: 8 -> 8, of which waited for: 2 -> 2; matrix products, arithmetic and copies ran while one was open for 1% -> 0% of each run, Pallas kernels for 14% -> 15%
where the time goes in v3:
time: 67 us; the launch traced here: 66.4 us
  starting transfers between devices  43.7 us (65%)
  Pallas kernels  13.3 us (20%)
  waiting for transfers between devices  4.63 us (7%)
  blocking collectives  4.5 us (7%)
    ppermute x4, starting transfers between devices, from_line(): return lax.ppermute(x, 'dp', pairs)  18.1 us
    ppermute x2, starting transfers between devices, from_core(): return lax.ppermute(x, 'dp', [(i, i ^ 1) for i in range(lines)])  10.8 us
    pallas_call x1, Pallas kernels, attend(): pl.pallas_call(attend_kernel, out_shape=jax.ShapeDtypeStruct((shards, (st...  8 us
    all_to_all x1, starting transfers between devices, body(): gathered = lax.all_to_all(packed, 'ctx', 0, 0, tiled=True)  7.72 us
    all_to_all x1, starting transfers between devices, body(): got = lax.all_to_all(partial, 'ctx', 0, 0, tiled=True)  7.08 us
    all_gather x1, blocking collectives, body(): lax.all_gather(value_up, 'dp', axis=1, tiled=True, axis_index_groups=[[2...  4.5 us
    ppermute x4, waiting for transfers between devices, from_line(): return lax.ppermute(x, 'dp', pairs)  3.5 us
    pallas_call x1, Pallas kernels, fresh_part(): pl.pallas_call(fresh_kernel, out_shape=(jax.ShapeDtypeStruct((count, LAT)...  2.08 us
  transfers between devices with their start and end apart: 8, of which 2 were waited for; matrix products, arithmetic and copies ran while one was open for 0% of the time, Pallas kernels for 15%

profile of v3, /device:TPU:1, one launch (start us, length us, event | category | flops | bytes accessed | tf_op | source)
XLA Modules:
  0.0 66.4 jit_solution(8792294104094693122)
XLA Ops:
  0.0 2.0 %pack_queries.1 = bf16[16,72,512]{2,1,0:T(8,128)(2,1)} custom-call(bf16[4,2,8,576]{3,2,1,0:T(8,128)(2,1)} %q_ref.3), custom_call_target="tpu_custom_call" | custom-call | tf_op jit(solution)/shard_map/pack_queries/pallas_call | solution.py:57
  2.0 7.7 %all-to-all-start = ((bf16[16,72,512]{2,1,0:T(8,128)(2,1)}), bf16[16,72,512]{2,1,0:T(8,128)(2,1)S(1)}, u32[]{:S(2)}, u32[]{:S(2)}) async-start(bf16[16,72,512]{2,1,0:T(8,128)(2,1)} %pack_queries.1), calls=%async_computation | async-start | bytes 2359296 | tf_op jit(solution)/shard_map/all_to_all | solution.py:397
  9.7 0.0 copy-done.3
  9.7 4.5 %all_gather.3 = bf16[8,32,128]{2,1,0:T(8,128)(2,1)S(1)} all-gather(bf16[8,16,128]{2,1,0:T(8,128)(2,1)S(1)} %copy-done.3), channel_id=1, replica_groups={{0,16},{32,48},{64,80},{96,112},{128,144},{160,176},{192,208},{224,240}..., dimensions={1}, use_global_device_ids=true | all-gather | bytes 98304 | tf_op jit(solution)/shard_map/all_gather | solution.py:399
  14.2 6.8 %collective-permute-start = (bf16[1,8,32,128]{3,2,1,0:T(8,128)(2,1)S(1)}, bf16[1,8,32,128]{3,2,1,0:T(8,128)(2,1)S(1)}, u32[]{:S(2)}, u32[]{:S(2)}) collective-permute-start(bf16[1,8,32,128]{3,2,1,0:T(8,128)(2,1)S(1)} %bitcast.2), channel_id=1, source_target_pairs={{128,0},{400,16},{160,32},{432,48},{192,64},{464,80},{224,96},{496... | collective-permute-start | bytes 196616 | tf_op jit(solution)/shard_map/ppermute | solution.py:390
  21.0 2.1 %fresh_part.1 = (f32[64,512]{1,0:T(8,128)}, f32[2,128]{1,0:T(2,128)}) custom-call(s32[2]{0:T(128)} %lengths_ref.1, bf16[4,2,8,576]{3,2,1,0:T(8,128)(2,1)} %q_ref.3, bf16[4,2,576]{2,1,0:T(2,128)(2,1)} %new_ref.1), custom_call_target="tpu_custom_call" | custom-call | tf_op jit(solution)/shard_map/fresh_part/pallas_call | solution.py:138
  23.1 3.5 %collective-permute-done = bf16[1,8,32,128]{3,2,1,0:T(8,128)(2,1)S(1)} collective-permute-done((bf16[1,8,32,128]{3,2,1,0:T(8,128)(2,1)S(1)}, bf16[1,8,32,128]{3,2,1,0:T(8,128)(2,1)S(1)}, u32[]{:S(2)}, u32[]{:S(2)}) %collective-permute-start) | collective-permute-done | bytes 65568 | tf_op jit(solution)/shard_map/ppermute | solution.py:390
  26.6 4.3 %collective-permute-start.1 = (bf16[2,8,32,128]{3,2,1,0:T(8,128)(2,1)S(1)}, bf16[2,8,32,128]{3,2,1,0:T(8,128)(2,1)S(1)}, u32[]{:S(2)}, u32[]{:S(2)}) collective-permute-start(bf16[2,8,32,128]{3,2,1,0:T(8,128)(2,1)S(1)} %pad_maximum_fusion), channel_id=1, source_target_pairs={{64,0},{464,16},{96,32},{496,48},{128,64},{16,80},{160,96},{48,112... | collective-permute-start | bytes 393224 | tf_op jit(solution)/shard_map/ppermute | solution.py:390
  30.9 0.0 all-to-all-done.q_ref
  30.9 0.0 copy-done.2
  30.9 8.0 %attend.1 = bf16[16,264,128]{2,1,0:T(8,128)(2,1)} custom-call(s32[2]{0:T(128)S(1)} %copy-done.2, bf16[16,72,512]{2,1,0:T(8,128)(2,1)S(1)} %all-to-all-done.q_ref, bf16[2,576,1536]{2,1,0:T(8,128)(2,1)} %bitcast.4), custom_call_target="tpu_custom_call" | custom-call | flops 3422552064 | bytes 5898240 | tf_op jit(solution)/shard_map/attend/pallas_call | solution.py:285
  39.0 0.0 copy-start.1
  39.0 0.0 collective-permute-done.1
  39.0 7.1 %all-to-all-start.1 = ((bf16[16,264,128]{2,1,0:T(8,128)(2,1)}), bf16[16,264,128]{2,1,0:T(8,128)(2,1)S(1)}, u32[]{:S(2)}, u32[]{:S(2)}) async-start(bf16[16,264,128]{2,1,0:T(8,128)(2,1)} %attend.1), calls=%async_computation.1 | async-start | bytes 2162688 | tf_op jit(solution)/shard_map/all_to_all | solution.py:411
  46.1 3.3 %collective-permute-start.2 = (bf16[4,8,32,128]{3,2,1,0:T(8,128)(2,1)S(1)}, bf16[4,8,32,128]{3,2,1,0:T(8,128)(2,1)S(1)}, u32[]{:S(2)}, u32[]{:S(2)}) collective-permute-start(bf16[4,8,32,128]{3,2,1,0:T(8,128)(2,1)S(1)} %constant_dynamic-update-slice_fusion.refs_0_), channel_id=1, source_target_pairs={{32,0},{496,16},{64,32},{16,48},{96,64},{48,80},{128,96},{80,112},... | collective-permute-start | bytes 786440 | tf_op jit(solution)/shard_map/ppermute | solution.py:390
  49.4 3.8 %collective-permute-start.3 = (bf16[1,8,32,128]{3,2,1,0:T(8,128)(2,1)S(1)}, bf16[1,8,32,128]{3,2,1,0:T(8,128)(2,1)S(1)}, u32[]{:S(2)}, u32[]{:S(2)}) collective-permute-start(bf16[1,8,32,128]{3,2,1,0:T(8,128)(2,1)S(1)} %slice.3), channel_id=1, source_target_pairs={{64,0},{464,16},{96,32},{496,48},{128,64},{16,80},{160,96},{48,112... | collective-permute-start | bytes 196616 | tf_op jit(solution)/shard_map/ppermute | solution.py:390
  53.2 8.0 %collective-permute-start.4 = (bf16[4,8,32,128]{3,2,1,0:T(8,128)(2,1)S(1)}, bf16[4,8,32,128]{3,2,1,0:T(8,128)(2,1)S(1)}, u32[]{:S(2)}, u32[]{:S(2)}) collective-permute-start(bf16[4,8,32,128]{3,2,1,0:T(8,128)(2,1)S(1)} %constant_dynamic-update-slice_fusion.refs_0_), channel_id=1, source_target_pairs={{0,16},{16,0},{32,48},{48,32},{64,80},{80,64},{96,112},{112,96},{1... | collective-permute-start | bytes 786440 | tf_op jit(solution)/shard_map/ppermute | solution.py:393
  61.1 0.0 collective-permute-done.3.refs_2_
  61.1 0.0 collective-permute-done.2.refs_1_
  61.2 2.8 %collective-permute-start.5 = (bf16[4,8,32,128]{3,2,1,0:T(8,128)(2,1)S(1)}, bf16[4,8,32,128]{3,2,1,0:T(8,128)(2,1)S(1)}, u32[]{:S(2)}, u32[]{:S(2)}) collective-permute-start(bf16[4,8,32,128]{3,2,1,0:T(8,128)(2,1)S(1)} %collective-permute-done.2.refs_1_), channel_id=1, source_target_pairs={{0,16},{16,0},{32,48},{48,32},{64,80},{80,64},{96,112},{112,96},{1... | collective-permute-start | bytes 786440 | tf_op jit(solution)/shard_map/ppermute | solution.py:393
  64.0 0.0 collective-permute-done.4.refs_3_
  64.0 1.1 %collective-permute-done.5.refs_4_ = bf16[4,8,32,128]{3,2,1,0:T(8,128)(2,1)S(1)} collective-permute-done((bf16[4,8,32,128]{3,2,1,0:T(8,128)(2,1)S(1)}, bf16[4,8,32,128]{3,2,1,0:T(8,128)(2,1)S(1)}, u32[]{:S(2)}, u32[]{:S(2)}) %collective-permute-start.5) | collective-permute-done | bytes 262176 | tf_op jit(solution)/shard_map/ppermute | solution.py:393
  65.2 0.0 all-to-all-done.1.got_ref
  65.2 1.2 %merge.1 = f32[4,2,8,128]{3,2,1,0:T(8,128)} custom-call(bf16[16,264,128]{2,1,0:T(8,128)(2,1)S(1)} %all-to-all-done.1.got_ref, f32[64,512]{1,0:T(8,128)S(1)} %copy-done, f32[2,128]{1,0:T(2,128)S(1)} %copy-done.1, bf16[4,8,32,128]{3,2,1,0:T(8,128)(2,1)S(1)} %constant_dynamic-update-slice_fusion.refs_0_, ...), custom_call_target="tpu_custom_call" | custom-call | tf_op jit(solution)/shard_map/merge/pallas_call | solution.py:367
  (9 shorter events, 0.1 us)
Async XLA Ops:
  2.0 7.7 %copy-start.3 = (bf16[8,16,128]{2,1,0:T(8,128)(2,1)S(1)}, bf16[8,16,128]{2,1,0:T(8,128)(2,1)}, u32[]{:S(2)}) copy-start(bf16[8,16,128]{2,1,0:T(8,128)(2,1)} %param.9) | copy-start | bytes 98308
  2.0 28.9 %copy-start.2 = (s32[2]{0:T(128)S(1)}, s32[2]{0:T(128)}, u32[]{:S(2)}) copy-start(s32[2]{0:T(128)} %lengths_ref.1) | copy-start | bytes 28
  2.0 28.9 %all-to-all-start = ((bf16[16,72,512]{2,1,0:T(8,128)(2,1)}), bf16[16,72,512]{2,1,0:T(8,128)(2,1)S(1)}, u32[]{:S(2)}, u32[]{:S(2)}) async-start(bf16[16,72,512]{2,1,0:T(8,128)(2,1)} %pack_queries.1), calls=%async_computation | async-start | bytes 2359296 | tf_op jit(solution)/shard_map/all_to_all | solution.py:397
  14.2 12.3 %collective-permute-start = (bf16[1,8,32,128]{3,2,1,0:T(8,128)(2,1)S(1)}, bf16[1,8,32,128]{3,2,1,0:T(8,128)(2,1)S(1)}, u32[]{:S(2)}, u32[]{:S(2)}) collective-permute-start(bf16[1,8,32,128]{3,2,1,0:T(8,128)(2,1)S(1)} %bitcast.2), channel_id=1, source_target_pairs={{128,0},{400,16},{160,32},{432,48},{192,64},{464,80},{224,96},{496... | collective-permute-start | bytes 196616 | tf_op jit(solution)/shard_map/ppermute | solution.py:390
  26.6 12.4 %collective-permute-start.1 = (bf16[2,8,32,128]{3,2,1,0:T(8,128)(2,1)S(1)}, bf16[2,8,32,128]{3,2,1,0:T(8,128)(2,1)S(1)}, u32[]{:S(2)}, u32[]{:S(2)}) collective-permute-start(bf16[2,8,32,128]{3,2,1,0:T(8,128)(2,1)S(1)} %pad_maximum_fusion), channel_id=1, source_target_pairs={{64,0},{464,16},{96,32},{496,48},{128,64},{16,80},{160,96},{48,112... | collective-permute-start | bytes 393224 | tf_op jit(solution)/shard_map/ppermute | solution.py:390
  39.0 26.2 %copy-start = (f32[64,512]{1,0:T(8,128)S(1)}, f32[64,512]{1,0:T(8,128)}, u32[]{:S(2)}) copy-start(f32[64,512]{1,0:T(8,128)} %get-tuple-element.24.fresh_ref) | copy-start | bytes 393220
  39.0 26.2 %copy-start.1 = (f32[2,128]{1,0:T(2,128)S(1)}, f32[2,128]{1,0:T(2,128)}, u32[]{:S(2)}) copy-start(f32[2,128]{1,0:T(2,128)} %get-tuple-element.25.fresh_lse_ref) | copy-start | bytes 3076
  39.0 26.2 %all-to-all-start.1 = ((bf16[16,264,128]{2,1,0:T(8,128)(2,1)}), bf16[16,264,128]{2,1,0:T(8,128)(2,1)S(1)}, u32[]{:S(2)}, u32[]{:S(2)}) async-start(bf16[16,264,128]{2,1,0:T(8,128)(2,1)} %attend.1), calls=%async_computation.1 | async-start | bytes 2162688 | tf_op jit(solution)/shard_map/all_to_all | solution.py:411
  46.1 15.0 %collective-permute-start.2 = (bf16[4,8,32,128]{3,2,1,0:T(8,128)(2,1)S(1)}, bf16[4,8,32,128]{3,2,1,0:T(8,128)(2,1)S(1)}, u32[]{:S(2)}, u32[]{:S(2)}) collective-permute-start(bf16[4,8,32,128]{3,2,1,0:T(8,128)(2,1)S(1)} %constant_dynamic-update-slice_fusion.refs_0_), channel_id=1, source_target_pairs={{32,0},{496,16},{64,32},{16,48},{96,64},{48,80},{128,96},{80,112},... | collective-permute-start | bytes 786440 | tf_op jit(solution)/shard_map/ppermute | solution.py:390
  49.4 11.7 %collective-permute-start.3 = (bf16[1,8,32,128]{3,2,1,0:T(8,128)(2,1)S(1)}, bf16[1,8,32,128]{3,2,1,0:T(8,128)(2,1)S(1)}, u32[]{:S(2)}, u32[]{:S(2)}) collective-permute-start(bf16[1,8,32,128]{3,2,1,0:T(8,128)(2,1)S(1)} %slice.3), channel_id=1, source_target_pairs={{64,0},{464,16},{96,32},{496,48},{128,64},{16,80},{160,96},{48,112... | collective-permute-start | bytes 196616 | tf_op jit(solution)/shard_map/ppermute | solution.py:390
  53.2 10.8 %collective-permute-start.4 = (bf16[4,8,32,128]{3,2,1,0:T(8,128)(2,1)S(1)}, bf16[4,8,32,128]{3,2,1,0:T(8,128)(2,1)S(1)}, u32[]{:S(2)}, u32[]{:S(2)}) collective-permute-start(bf16[4,8,32,128]{3,2,1,0:T(8,128)(2,1)S(1)} %constant_dynamic-update-slice_fusion.refs_0_), channel_id=1, source_target_pairs={{0,16},{16,0},{32,48},{48,32},{64,80},{80,64},{96,112},{112,96},{1... | collective-permute-start | bytes 786440 | tf_op jit(solution)/shard_map/ppermute | solution.py:393
  61.2 4.0 %collective-permute-start.5 = (bf16[4,8,32,128]{3,2,1,0:T(8,128)(2,1)S(1)}, bf16[4,8,32,128]{3,2,1,0:T(8,128)(2,1)S(1)}, u32[]{:S(2)}, u32[]{:S(2)}) collective-permute-start(bf16[4,8,32,128]{3,2,1,0:T(8,128)(2,1)S(1)} %collective-permute-done.2.refs_1_), channel_id=1, source_target_pairs={{0,16},{16,0},{32,48},{48,32},{64,80},{80,64},{96,112},{112,96},{1... | collective-permute-start | bytes 786440 | tf_op jit(solution)/shard_map/ppermute | solution.py:393

commit v4 on v3

--- a/solution.py
+++ b/solution.py
@@ -164,8 +164,8 @@
     copies = [
         [
             pltpu.make_async_copy(
-                cache_ref.at[r, pl.ds(part * deep, deep)],
-                keys_ref.at[r, pl.ds(part * deep, deep)],
+                cache_ref.at[r, pl.ds(part * 256, 256 + 64 * part)],
+                keys_ref.at[r, pl.ds(part * 256, 256 + 64 * part)],
                 sems.at[r, part],
             )
             for part in range(PARTS)
@@ -209,10 +209,23 @@
         ),
     ]
 
+    def partial_score(r, lo, hi, fresh):
+        for first in range(0, span, CHUNK):
+            part = jnp.dot(
+                q_scr[r, :, lo:hi], keys_ref[r, lo:hi, first : first + CHUNK], preferred_element_type=F32
+            )
+            if not fresh:
+                part += s_scr[r, :, first : first + CHUNK]
+            s_scr[r, :, first : first + CHUNK] = part
+
     def score(r, first, top):
-        part = jnp.dot(
-            q_scr[r], keys_ref[r, :, first : first + CHUNK], preferred_element_type=F32
-        )
+        if r == 0:
+            part = s_scr[r, :, first : first + CHUNK]
+            part += jnp.dot(q_scr[r, :, 256:], keys_ref[r, 256:, first : first + CHUNK], preferred_element_type=F32)
+        else:
+            part = jnp.dot(
+                q_scr[r], keys_ref[r, :, first : first + CHUNK], preferred_element_type=F32
+            )
         s_scr[r, :, first : first + CHUNK] = part
         for lanes in range(0, CHUNK, 128):
             block = part[:, lanes : lanes + 128]
@@ -244,8 +257,10 @@
     levels = []
     totals = [None] * rows
     for r in range(rows):
-        for copy in copies[r]:
-            copy.wait()
+        copies[r][0].wait()
+        if r == 0:
+            partial_score(0, 0, 256, True)
+        copies[r][1].wait()
         if r + 1 < rows:
             for copy in copies[r + 1]:
                 copy.start()
@@ -316,11 +331,17 @@
     chips = lax.axis_size("dp") // 2
     z = line // 2
     own = 1 - 2 * (line % 2)
-    for ref, mine, spans in zip(up_refs, (1, 1, 1, -1, -1), offsets):
-        depth = ref.shape[2]
+    depth = up_refs[0].shape[2]
+    spare = up_refs[1].shape[0] - 1
+
+    def place(offset, block):
+        chip = (z + own * offset + chips) % chips
+        up[:, pl.ds(pl.multiple_of(chip * depth, depth), depth), :] = block
+
+    for ref, mine, spans in zip(up_refs, (1, 1, -1, -1), offsets):
         for b, offset in enumerate(spans):
-            chip = (z + own * (mine * offset) + chips) % chips
-            up[:, pl.ds(pl.multiple_of(chip * depth, depth), depth), :] = ref[b]
+            place(mine * offset, ref[b])
+    place(chips // 2, jnp.where(own < 0, up_refs[1][spare], up_refs[3][spare]))
     tail = got_ref[:, LAT // 128 * count :, :].astype(F32)
     sub = lax.broadcasted_iota(jnp.int32, (per_row, 128), 0)
     lane = lax.broadcasted_iota(jnp.int32, (per_row, 128), 1)
@@ -381,12 +402,12 @@
     lines = lax.axis_size("dp")
     chips = lines // 2
 
-    def from_line(x, reach):
+    def from_line(x, reach, cores=(0, 1)):
         pairs = []
         for line in range(lines):
             z, core = line // 2, line % 2
-            sign = 1 - 2 * core
-            pairs.append((((z + sign * reach) % chips) * 2 + core, line))
+            if core in cores:
+                pairs.append(((z + (1 - 2 * core) * reach) % chips * 2 + core, line))
         return lax.ppermute(x, "dp", pairs)
 
     def from_core(x):
@@ -411,11 +432,12 @@
     got = lax.all_to_all(partial, "ctx", 0, 0, tiled=True)
     held = jnp.concatenate([held, second], axis=0)
     third = from_line(held, 1)
-    eighth = from_line(second[-1:], 2)
+    eighth = from_line(second[-1:], 2, (1,))
     third, eighth = lax.optimization_barrier((third, eighth))
-    ups = (held, third, eighth, from_core(held), from_core(third))
+    third = jnp.concatenate([third, eighth], axis=0)
+    ups = (held, third, from_core(held), from_core(third))
     even, odd = (0, 4, 2, 6), (1, 5, 3, 7)
-    return merge(got, fresh, fresh_lse, ups, (even, odd, (8,), even, odd), steps, rows)
+    return merge(got, fresh, fresh_lse, ups, (even, odd, even, odd), steps, rows)
 
 
 def solution(mesh):

time: 67 us -> 66 us (0.985)
  starting transfers between devices: 43.7 us -> 38.3 us
  waiting for transfers between devices: 4.63 us -> 9.22 us
    ppermute x2, starting transfers between devices: 10.8 us -> 5.53 us  [from_core(): return lax.ppermute(x, 'dp', [(i, i ^ 1) for i in range(lines)])]
    ppermute x4, waiting for transfers between devices: 3.5 us -> 7.72 us  [from_line(): return lax.ppermute(x, 'dp', pairs)]
  transfers between devices with their start and end apart: 8 -> 8, of which waited for: 2 -> 3; matrix products, arithmetic and copies ran while one was open for 0% -> 0% of each run, Pallas kernels for 15% -> 15%
where the time goes in v4:
time: 66 us; the launch traced here: 65.4 us
  starting transfers between devices  38.3 us (58%)
  Pallas kernels  13.1 us (20%)
  waiting for transfers between devices  9.22 us (14%)
  blocking collectives  4.5 us (7%)
    ppermute x4, starting transfers between devices, from_line(): return lax.ppermute(x, 'dp', pairs)  18.1 us
    pallas_call x1, Pallas kernels, attend(): pl.pallas_call(attend_kernel, out_shape=jax.ShapeDtypeStruct((shards, (st...  7.8 us
    all_to_all x1, starting transfers between devices, body(): gathered = lax.all_to_all(packed, 'ctx', 0, 0, tiled=True)  7.72 us
    ppermute x4, waiting for transfers between devices, from_line(): return lax.ppermute(x, 'dp', pairs)  7.72 us
    all_to_all x1, starting transfers between devices, body(): got = lax.all_to_all(partial, 'ctx', 0, 0, tiled=True)  6.94 us
    ppermute x2, starting transfers between devices, from_core(): return lax.ppermute(x, 'dp', [(i, i ^ 1) for i in range(lines)])  5.53 us
    all_gather x1, blocking collectives, body(): lax.all_gather(value_up, 'dp', axis=1, tiled=True, axis_index_groups=[[2...  4.5 us
    pallas_call x1, Pallas kernels, fresh_part(): pl.pallas_call(fresh_kernel, out_shape=(jax.ShapeDtypeStruct((count, LAT)...  2.08 us
  transfers between devices with their start and end apart: 8, of which 3 were waited for; matrix products, arithmetic and copies ran while one was open for 0% of the time, Pallas kernels for 15%

profile of v4, /device:TPU:1, one launch (start us, length us, event | category | flops | bytes accessed | tf_op | source)
XLA Modules:
  0.0 65.4 jit_solution(7658455857393043264)
XLA Ops:
  0.0 2.0 %pack_queries.1 = bf16[16,72,512]{2,1,0:T(8,128)(2,1)} custom-call(bf16[4,2,8,576]{3,2,1,0:T(8,128)(2,1)} %q_ref.3), custom_call_target="tpu_custom_call" | custom-call | tf_op jit(solution)/shard_map/pack_queries/pallas_call | solution.py:57
  2.0 7.7 %all-to-all-start = ((bf16[16,72,512]{2,1,0:T(8,128)(2,1)}), bf16[16,72,512]{2,1,0:T(8,128)(2,1)S(1)}, u32[]{:S(2)}, u32[]{:S(2)}) async-start(bf16[16,72,512]{2,1,0:T(8,128)(2,1)} %pack_queries.1), calls=%async_computation | async-start | bytes 2359296 | tf_op jit(solution)/shard_map/all_to_all | solution.py:418
  9.7 0.0 copy-done.3
  9.7 4.5 %all_gather.3 = bf16[8,32,128]{2,1,0:T(8,128)(2,1)S(1)} all-gather(bf16[8,16,128]{2,1,0:T(8,128)(2,1)S(1)} %copy-done.3), channel_id=1, replica_groups={{0,16},{32,48},{64,80},{96,112},{128,144},{160,176},{192,208},{224,240}..., dimensions={1}, use_global_device_ids=true | all-gather | bytes 98304 | tf_op jit(solution)/shard_map/all_gather | solution.py:420
  14.2 6.8 %collective-permute-start = (bf16[1,8,32,128]{3,2,1,0:T(8,128)(2,1)S(1)}, bf16[1,8,32,128]{3,2,1,0:T(8,128)(2,1)S(1)}, u32[]{:S(2)}, u32[]{:S(2)}) collective-permute-start(bf16[1,8,32,128]{3,2,1,0:T(8,128)(2,1)S(1)} %bitcast.2), channel_id=1, source_target_pairs={{128,0},{400,16},{160,32},{432,48},{192,64},{464,80},{224,96},{496... | collective-permute-start | bytes 196616 | tf_op jit(solution)/shard_map/ppermute | solution.py:411
  21.0 2.1 %fresh_part.1 = (f32[64,512]{1,0:T(8,128)}, f32[2,128]{1,0:T(2,128)}) custom-call(s32[2]{0:T(128)} %lengths_ref.1, bf16[4,2,8,576]{3,2,1,0:T(8,128)(2,1)} %q_ref.3, bf16[4,2,576]{2,1,0:T(2,128)(2,1)} %new_ref.1), custom_call_target="tpu_custom_call" | custom-call | tf_op jit(solution)/shard_map/fresh_part/pallas_call | solution.py:138
  23.1 3.5 %collective-permute-done = bf16[1,8,32,128]{3,2,1,0:T(8,128)(2,1)S(1)} collective-permute-done((bf16[1,8,32,128]{3,2,1,0:T(8,128)(2,1)S(1)}, bf16[1,8,32,128]{3,2,1,0:T(8,128)(2,1)S(1)}, u32[]{:S(2)}, u32[]{:S(2)}) %collective-permute-start) | collective-permute-done | bytes 65568 | tf_op jit(solution)/shard_map/ppermute | solution.py:411
  26.6 4.3 %collective-permute-start.1 = (bf16[2,8,32,128]{3,2,1,0:T(8,128)(2,1)S(1)}, bf16[2,8,32,128]{3,2,1,0:T(8,128)(2,1)S(1)}, u32[]{:S(2)}, u32[]{:S(2)}) collective-permute-start(bf16[2,8,32,128]{3,2,1,0:T(8,128)(2,1)S(1)} %pad_maximum_fusion), channel_id=1, source_target_pairs={{64,0},{464,16},{96,32},{496,48},{128,64},{16,80},{160,96},{48,112... | collective-permute-start | bytes 393224 | tf_op jit(solution)/shard_map/ppermute | solution.py:411
  30.9 0.0 all-to-all-done.q_ref
  30.9 0.0 copy-done.2
  30.9 7.8 %attend.1 = bf16[16,264,128]{2,1,0:T(8,128)(2,1)} custom-call(s32[2]{0:T(128)S(1)} %copy-done.2, bf16[16,72,512]{2,1,0:T(8,128)(2,1)S(1)} %all-to-all-done.q_ref, bf16[2,576,1536]{2,1,0:T(8,128)(2,1)} %bitcast.4), custom_call_target="tpu_custom_call" | custom-call | flops 3422552064 | bytes 5898240 | tf_op jit(solution)/shard_map/attend/pallas_call | solution.py:300
  38.8 0.0 collective-permute-done.1
  38.8 6.9 %all-to-all-start.1 = ((bf16[16,264,128]{2,1,0:T(8,128)(2,1)}), bf16[16,264,128]{2,1,0:T(8,128)(2,1)S(1)}, u32[]{:S(2)}, u32[]{:S(2)}) async-start(bf16[16,264,128]{2,1,0:T(8,128)(2,1)} %attend.1), calls=%async_computation.1 | async-start | bytes 2162688 | tf_op jit(solution)/shard_map/all_to_all | solution.py:432
  45.7 0.0 copy-start.1
  45.8 3.3 %collective-permute-start.2 = (bf16[4,8,32,128]{3,2,1,0:T(8,128)(2,1)S(1)}, bf16[4,8,32,128]{3,2,1,0:T(8,128)(2,1)S(1)}, u32[]{:S(2)}, u32[]{:S(2)}) collective-permute-start(bf16[4,8,32,128]{3,2,1,0:T(8,128)(2,1)S(1)} %constant_dynamic-update-slice_fusion.refs_0_), channel_id=1, source_target_pairs={{32,0},{496,16},{64,32},{16,48},{96,64},{48,80},{128,96},{80,112},... | collective-permute-start | bytes 786440 | tf_op jit(solution)/shard_map/ppermute | solution.py:411
  49.1 3.8 %collective-permute-start.3 = (bf16[1,8,32,128]{3,2,1,0:T(8,128)(2,1)S(1)}, bf16[1,8,32,128]{3,2,1,0:T(8,128)(2,1)S(1)}, u32[]{:S(2)}, u32[]{:S(2)}) collective-permute-start(bf16[1,8,32,128]{3,2,1,0:T(8,128)(2,1)S(1)} %slice.3), channel_id=1, source_target_pairs={{464,16},{496,48},{16,80},{48,112},{80,144},{112,176},{144,208},{1... | collective-permute-start | bytes 196616 | tf_op jit(solution)/shard_map/ppermute | solution.py:411
  52.9 4.2 %collective-permute-done.3 = bf16[1,8,32,128]{3,2,1,0:T(8,128)(2,1)S(1)} collective-permute-done((bf16[1,8,32,128]{3,2,1,0:T(8,128)(2,1)S(1)}, bf16[1,8,32,128]{3,2,1,0:T(8,128)(2,1)S(1)}, u32[]{:S(2)}, u32[]{:S(2)}) %collective-permute-start.3) | collective-permute-done | bytes 65568 | tf_op jit(solution)/shard_map/ppermute | solution.py:411
  57.1 0.0 collective-permute-done.2
  57.1 3.6 %collective-permute-start.5 = (bf16[5,8,32,128]{3,2,1,0:T(8,128)(2,1)S(1)}, bf16[5,8,32,128]{3,2,1,0:T(8,128)(2,1)S(1)}, u32[]{:S(2)}, u32[]{:S(2)}) collective-permute-start(bf16[5,8,32,128]{3,2,1,0:T(8,128)(2,1)S(1)} %constant_dynamic-update-slice_fusion.2.refs_1_), channel_id=1, source_target_pairs={{0,16},{16,0},{32,48},{48,32},{64,80},{80,64},{96,112},{112,96},{1... | collective-permute-start | bytes 983048 | tf_op jit(solution)/shard_map/ppermute | solution.py:414
  60.7 1.9 %collective-permute-start.4 = (bf16[4,8,32,128]{3,2,1,0:T(8,128)(2,1)S(1)}, bf16[4,8,32,128]{3,2,1,0:T(8,128)(2,1)S(1)}, u32[]{:S(2)}, u32[]{:S(2)}) collective-permute-start(bf16[4,8,32,128]{3,2,1,0:T(8,128)(2,1)S(1)} %constant_dynamic-update-slice_fusion.refs_0_), channel_id=1, source_target_pairs={{0,16},{16,0},{32,48},{48,32},{64,80},{80,64},{96,112},{112,96},{1... | collective-permute-start | bytes 786440 | tf_op jit(solution)/shard_map/ppermute | solution.py:414
  62.7 1.5 %collective-permute-done.4.refs_2_ = bf16[4,8,32,128]{3,2,1,0:T(8,128)(2,1)S(1)} collective-permute-done((bf16[4,8,32,128]{3,2,1,0:T(8,128)(2,1)S(1)}, bf16[4,8,32,128]{3,2,1,0:T(8,128)(2,1)S(1)}, u32[]{:S(2)}, u32[]{:S(2)}) %collective-permute-start.4) | collective-permute-done | bytes 262176 | tf_op jit(solution)/shard_map/ppermute | solution.py:414
  64.2 0.0 collective-permute-done.5.refs_3_
  64.2 0.0 all-to-all-done.1.got_ref
  64.2 1.2 %merge.1 = f32[4,2,8,128]{3,2,1,0:T(8,128)} custom-call(bf16[16,264,128]{2,1,0:T(8,128)(2,1)S(1)} %all-to-all-done.1.got_ref, f32[64,512]{1,0:T(8,128)S(1)} %copy-done, f32[2,128]{1,0:T(2,128)S(1)} %copy-done.1, bf16[4,8,32,128]{3,2,1,0:T(8,128)(2,1)S(1)} %constant_dynamic-update-slice_fusion.refs_0_, ...), custom_call_target="tpu_custom_call" | custom-call | tf_op jit(solution)/shard_map/merge/pallas_call | solution.py:388
  (11 shorter events, 0.1 us)
Async XLA Ops:
  2.0 7.7 %copy-start.3 = (bf16[8,16,128]{2,1,0:T(8,128)(2,1)S(1)}, bf16[8,16,128]{2,1,0:T(8,128)(2,1)}, u32[]{:S(2)}) copy-start(bf16[8,16,128]{2,1,0:T(8,128)(2,1)} %param.9) | copy-start | bytes 98308
  2.0 28.9 %copy-start.2 = (s32[2]{0:T(128)S(1)}, s32[2]{0:T(128)}, u32[]{:S(2)}) copy-start(s32[2]{0:T(128)} %lengths_ref.1) | copy-start | bytes 28
  2.0 28.9 %all-to-all-start = ((bf16[16,72,512]{2,1,0:T(8,128)(2,1)}), bf16[16,72,512]{2,1,0:T(8,128)(2,1)S(1)}, u32[]{:S(2)}, u32[]{:S(2)}) async-start(bf16[16,72,512]{2,1,0:T(8,128)(2,1)} %pack_queries.1), calls=%async_computation | async-start | bytes 2359296 | tf_op jit(solution)/shard_map/all_to_all | solution.py:418
  14.2 12.3 %collective-permute-start = (bf16[1,8,32,128]{3,2,1,0:T(8,128)(2,1)S(1)}, bf16[1,8,32,128]{3,2,1,0:T(8,128)(2,1)S(1)}, u32[]{:S(2)}, u32[]{:S(2)}) collective-permute-start(bf16[1,8,32,128]{3,2,1,0:T(8,128)(2,1)S(1)} %bitcast.2), channel_id=1, source_target_pairs={{128,0},{400,16},{160,32},{432,48},{192,64},{464,80},{224,96},{496... | collective-permute-start | bytes 196616 | tf_op jit(solution)/shard_map/ppermute | solution.py:411
  26.6 12.1 %collective-permute-start.1 = (bf16[2,8,32,128]{3,2,1,0:T(8,128)(2,1)S(1)}, bf16[2,8,32,128]{3,2,1,0:T(8,128)(2,1)S(1)}, u32[]{:S(2)}, u32[]{:S(2)}) collective-permute-start(bf16[2,8,32,128]{3,2,1,0:T(8,128)(2,1)S(1)} %pad_maximum_fusion), channel_id=1, source_target_pairs={{64,0},{464,16},{96,32},{496,48},{128,64},{16,80},{160,96},{48,112... | collective-permute-start | bytes 393224 | tf_op jit(solution)/shard_map/ppermute | solution.py:411
  38.8 25.4 %all-to-all-start.1 = ((bf16[16,264,128]{2,1,0:T(8,128)(2,1)}), bf16[16,264,128]{2,1,0:T(8,128)(2,1)S(1)}, u32[]{:S(2)}, u32[]{:S(2)}) async-start(bf16[16,264,128]{2,1,0:T(8,128)(2,1)} %attend.1), calls=%async_computation.1 | async-start | bytes 2162688 | tf_op jit(solution)/shard_map/all_to_all | solution.py:432
  45.7 18.5 %copy-start = (f32[64,512]{1,0:T(8,128)S(1)}, f32[64,512]{1,0:T(8,128)}, u32[]{:S(2)}) copy-start(f32[64,512]{1,0:T(8,128)} %get-tuple-element.24.fresh_ref) | copy-start | bytes 393220
  45.7 18.5 %copy-start.1 = (f32[2,128]{1,0:T(2,128)S(1)}, f32[2,128]{1,0:T(2,128)}, u32[]{:S(2)}) copy-start(f32[2,128]{1,0:T(2,128)} %get-tuple-element.25.fresh_lse_ref) | copy-start | bytes 3076
  45.8 11.3 %collective-permute-start.2 = (bf16[4,8,32,128]{3,2,1,0:T(8,128)(2,1)S(1)}, bf16[4,8,32,128]{3,2,1,0:T(8,128)(2,1)S(1)}, u32[]{:S(2)}, u32[]{:S(2)}) collective-permute-start(bf16[4,8,32,128]{3,2,1,0:T(8,128)(2,1)S(1)} %constant_dynamic-update-slice_fusion.refs_0_), channel_id=1, source_target_pairs={{32,0},{496,16},{64,32},{16,48},{96,64},{48,80},{128,96},{80,112},... | collective-permute-start | bytes 786440 | tf_op jit(solution)/shard_map/ppermute | solution.py:411
  49.1 8.0 %collective-permute-start.3 = (bf16[1,8,32,128]{3,2,1,0:T(8,128)(2,1)S(1)}, bf16[1,8,32,128]{3,2,1,0:T(8,128)(2,1)S(1)}, u32[]{:S(2)}, u32[]{:S(2)}) collective-permute-start(bf16[1,8,32,128]{3,2,1,0:T(8,128)(2,1)S(1)} %slice.3), channel_id=1, source_target_pairs={{464,16},{496,48},{16,80},{48,112},{80,144},{112,176},{144,208},{1... | collective-permute-start | bytes 196616 | tf_op jit(solution)/shard_map/ppermute | solution.py:411
  57.1 7.1 %collective-permute-start.5 = (bf16[5,8,32,128]{3,2,1,0:T(8,128)(2,1)S(1)}, bf16[5,8,32,128]{3,2,1,0:T(8,128)(2,1)S(1)}, u32[]{:S(2)}, u32[]{:S(2)}) collective-permute-start(bf16[5,8,32,128]{3,2,1,0:T(8,128)(2,1)S(1)} %constant_dynamic-update-slice_fusion.2.refs_1_), channel_id=1, source_target_pairs={{0,16},{16,0},{32,48},{48,32},{64,80},{80,64},{96,112},{112,96},{1... | collective-permute-start | bytes 983048 | tf_op jit(solution)/shard_map/ppermute | solution.py:414
  60.7 3.4 %collective-permute-start.4 = (bf16[4,8,32,128]{3,2,1,0:T(8,128)(2,1)S(1)}, bf16[4,8,32,128]{3,2,1,0:T(8,128)(2,1)S(1)}, u32[]{:S(2)}, u32[]{:S(2)}) collective-permute-start(bf16[4,8,32,128]{3,2,1,0:T(8,128)(2,1)S(1)} %constant_dynamic-update-slice_fusion.refs_0_), channel_id=1, source_target_pairs={{0,16},{16,0},{32,48},{48,32},{64,80},{80,64},{96,112},{112,96},{1... | collective-permute-start | bytes 786440 | tf_op jit(solution)/shard_map/ppermute | solution.py:414

commit v5 on v4

--- a/solution.py
+++ b/solution.py
@@ -433,9 +433,10 @@
     held = jnp.concatenate([held, second], axis=0)
     third = from_line(held, 1)
     eighth = from_line(second[-1:], 2, (1,))
-    third, eighth = lax.optimization_barrier((third, eighth))
+    eighth, held = lax.optimization_barrier((eighth, held))
+    third, eighth, other = lax.optimization_barrier((third, eighth, from_core(held)))
     third = jnp.concatenate([third, eighth], axis=0)
-    ups = (held, third, from_core(held), from_core(third))
+    ups = (held, third, other, from_core(third))
     even, odd = (0, 4, 2, 6), (1, 5, 3, 7)
     return merge(got, fresh, fresh_lse, ups, (even, odd, even, odd), steps, rows)
 

time: 66 us -> 65.4 us (level)
  the two profiles are of different devices: /device:TPU:1 before, /device:TPU:64 now
where the time goes in v5:
time: 65.4 us; the launch traced here: 64.8 us
  starting transfers between devices  39.8 us (61%)
  Pallas kernels  13.1 us (20%)
  waiting for transfers between devices  9.7 us (15%)
  blocking collectives  1.85 us (3%)
    ppermute x4, starting transfers between devices, from_line(): return lax.ppermute(x, 'dp', pairs)  22 us
    pallas_call x1, Pallas kernels, attend(): pl.pallas_call(attend_kernel, out_shape=jax.ShapeDtypeStruct((shards, (st...  7.79 us
    all_to_all x1, starting transfers between devices, body(): gathered = lax.all_to_all(packed, 'ctx', 0, 0, tiled=True)  7.17 us
    all_to_all x1, starting transfers between devices, body(): got = lax.all_to_all(partial, 'ctx', 0, 0, tiled=True)  6.3 us
    all_to_all x1, waiting for transfers between devices, body(): got = lax.all_to_all(partial, 'ctx', 0, 0, tiled=True)  5.75 us
    ppermute x2, starting transfers between devices, from_core(): return lax.ppermute(x, 'dp', [(i, i ^ 1) for i in range(lines)])  4.37 us
    pallas_call x1, Pallas kernels, fresh_part(): pl.pallas_call(fresh_kernel, out_shape=(jax.ShapeDtypeStruct((count, LAT)...  2.09 us
    pallas_call x1, Pallas kernels, pack_queries(): pl.pallas_call(pack_kernel, out_shape=jax.ShapeDtypeStruct((shards, count...  2.01 us
  transfers between devices with their start and end apart: 8, of which 4 were waited for; matrix products, arithmetic and copies ran while one was open for 0% of the time, Pallas kernels for 15%

profile of v5, /device:TPU:64, one launch (start us, length us, event | category | flops | bytes accessed | tf_op | source)
XLA Modules:
  0.0 64.8 jit_solution(4225366313518299884)
XLA Ops:
  0.0 2.0 %pack_queries.1 = bf16[16,72,512]{2,1,0:T(8,128)(2,1)} custom-call(bf16[4,2,8,576]{3,2,1,0:T(8,128)(2,1)} %q_ref.3), custom_call_target="tpu_custom_call" | custom-call | tf_op jit(solution)/shard_map/pack_queries/pallas_call | solution.py:57
  2.0 7.2 %all-to-all-start = ((bf16[16,72,512]{2,1,0:T(8,128)(2,1)}), bf16[16,72,512]{2,1,0:T(8,128)(2,1)S(1)}, u32[]{:S(2)}, u32[]{:S(2)}) async-start(bf16[16,72,512]{2,1,0:T(8,128)(2,1)} %pack_queries.1), calls=%async_computation | async-start | bytes 2359296 | tf_op jit(solution)/shard_map/all_to_all | solution.py:418
  9.2 0.0 copy-done.3
  9.2 1.9 %all_gather.3 = bf16[8,32,128]{2,1,0:T(8,128)(2,1)S(1)} all-gather(bf16[8,16,128]{2,1,0:T(8,128)(2,1)S(1)} %copy-done.3), channel_id=1, replica_groups={{0,16},{32,48},{64,80},{96,112},{128,144},{160,176},{192,208},{224,240}..., dimensions={1}, use_global_device_ids=true | all-gather | bytes 98304 | tf_op jit(solution)/shard_map/all_gather | solution.py:420
  11.0 10.9 %collective-permute-start = (bf16[1,8,32,128]{3,2,1,0:T(8,128)(2,1)S(1)}, bf16[1,8,32,128]{3,2,1,0:T(8,128)(2,1)S(1)}, u32[]{:S(2)}, u32[]{:S(2)}) collective-permute-start(bf16[1,8,32,128]{3,2,1,0:T(8,128)(2,1)S(1)} %bitcast.2), channel_id=1, source_target_pairs={{128,0},{400,16},{160,32},{432,48},{192,64},{464,80},{224,96},{496... | collective-permute-start | bytes 196616 | tf_op jit(solution)/shard_map/ppermute | solution.py:411
  22.0 2.1 %fresh_part.1 = (f32[64,512]{1,0:T(8,128)}, f32[2,128]{1,0:T(2,128)}) custom-call(s32[2]{0:T(128)} %lengths_ref.1, bf16[4,2,8,576]{3,2,1,0:T(8,128)(2,1)} %q_ref.3, bf16[4,2,576]{2,1,0:T(2,128)(2,1)} %new_ref.1), custom_call_target="tpu_custom_call" | custom-call | tf_op jit(solution)/shard_map/fresh_part/pallas_call | solution.py:138
  24.1 0.0 collective-permute-done
  24.1 3.4 %collective-permute-start.1 = (bf16[2,8,32,128]{3,2,1,0:T(8,128)(2,1)S(1)}, bf16[2,8,32,128]{3,2,1,0:T(8,128)(2,1)S(1)}, u32[]{:S(2)}, u32[]{:S(2)}) collective-permute-start(bf16[2,8,32,128]{3,2,1,0:T(8,128)(2,1)S(1)} %pad_maximum_fusion), channel_id=1, source_target_pairs={{64,0},{464,16},{96,32},{496,48},{128,64},{16,80},{160,96},{48,112... | collective-permute-start | bytes 393224 | tf_op jit(solution)/shard_map/ppermute | solution.py:411
  27.5 0.9 %all-to-all-done.q_ref = bf16[16,72,512]{2,1,0:T(8,128)(2,1)S(1)} async-done(((bf16[16,72,512]{2,1,0:T(8,128)(2,1)}), bf16[16,72,512]{2,1,0:T(8,128)(2,1)S(1)}, u32[]{:S(2)}, u32[]{:S(2)}) %all-to-all-start) | async-done | bytes 1179680 | tf_op jit(solution)/shard_map/all_to_all | solution.py:418
  28.4 7.8 %attend.1 = bf16[16,264,128]{2,1,0:T(8,128)(2,1)} custom-call(s32[2]{0:T(128)S(1)} %copy-done.2, bf16[16,72,512]{2,1,0:T(8,128)(2,1)S(1)} %all-to-all-done.q_ref, bf16[2,576,1536]{2,1,0:T(8,128)(2,1)} %bitcast.4), custom_call_target="tpu_custom_call" | custom-call | flops 3422552064 | bytes 5898240 | tf_op jit(solution)/shard_map/attend/pallas_call | solution.py:300
  36.2 0.0 collective-permute-done.1
  36.2 6.3 %all-to-all-start.1 = ((bf16[16,264,128]{2,1,0:T(8,128)(2,1)}), bf16[16,264,128]{2,1,0:T(8,128)(2,1)S(1)}, u32[]{:S(2)}, u32[]{:S(2)}) async-start(bf16[16,264,128]{2,1,0:T(8,128)(2,1)} %attend.1), calls=%async_computation.1 | async-start | bytes 2162688 | tf_op jit(solution)/shard_map/all_to_all | solution.py:432
  42.5 0.0 copy-start.1
  42.6 0.8 %collective-permute-start.2 = (bf16[1,8,32,128]{3,2,1,0:T(8,128)(2,1)S(1)}, bf16[1,8,32,128]{3,2,1,0:T(8,128)(2,1)S(1)}, u32[]{:S(2)}, u32[]{:S(2)}) collective-permute-start(bf16[1,8,32,128]{3,2,1,0:T(8,128)(2,1)S(1)} %slice.3), channel_id=1, source_target_pairs={{464,16},{496,48},{16,80},{48,112},{80,144},{112,176},{144,208},{1... | collective-permute-start | bytes 196616 | tf_op jit(solution)/shard_map/ppermute | solution.py:411
  43.4 6.9 %collective-permute-start.3 = (bf16[4,8,32,128]{3,2,1,0:T(8,128)(2,1)S(1)}, bf16[4,8,32,128]{3,2,1,0:T(8,128)(2,1)S(1)}, u32[]{:S(2)}, u32[]{:S(2)}) collective-permute-start(bf16[4,8,32,128]{3,2,1,0:T(8,128)(2,1)S(1)} %constant_dynamic-update-slice_fusion.refs_0_), channel_id=1, source_target_pairs={{32,0},{496,16},{64,32},{16,48},{96,64},{48,80},{128,96},{80,112},... | collective-permute-start | bytes 786440 | tf_op jit(solution)/shard_map/ppermute | solution.py:411
  50.4 0.0 collective-permute-done.2
  50.4 2.3 %collective-permute-start.4 = (bf16[4,8,32,128]{3,2,1,0:T(8,128)(2,1)S(1)}, bf16[4,8,32,128]{3,2,1,0:T(8,128)(2,1)S(1)}, u32[]{:S(2)}, u32[]{:S(2)}) collective-permute-start(bf16[4,8,32,128]{3,2,1,0:T(8,128)(2,1)S(1)} %constant_dynamic-update-slice_fusion.refs_0_), channel_id=1, source_target_pairs={{0,16},{16,0},{32,48},{48,32},{64,80},{80,64},{96,112},{112,96},{1... | collective-permute-start | bytes 786440 | tf_op jit(solution)/shard_map/ppermute | solution.py:414
  52.7 1.5 %collective-permute-done.3 = bf16[4,8,32,128]{3,2,1,0:T(8,128)(2,1)S(1)} collective-permute-done((bf16[4,8,32,128]{3,2,1,0:T(8,128)(2,1)S(1)}, bf16[4,8,32,128]{3,2,1,0:T(8,128)(2,1)S(1)}, u32[]{:S(2)}, u32[]{:S(2)}) %collective-permute-start.3) | collective-permute-done | bytes 262176 | tf_op jit(solution)/shard_map/ppermute | solution.py:411
  54.2 0.0 collective-permute-done.4.refs_2_
  54.3 2.1 %collective-permute-start.5 = (bf16[5,8,32,128]{3,2,1,0:T(8,128)(2,1)S(1)}, bf16[5,8,32,128]{3,2,1,0:T(8,128)(2,1)S(1)}, u32[]{:S(2)}, u32[]{:S(2)}) collective-permute-start(bf16[5,8,32,128]{3,2,1,0:T(8,128)(2,1)S(1)} %constant_dynamic-update-slice_fusion.2.refs_1_), channel_id=1, source_target_pairs={{0,16},{16,0},{32,48},{48,32},{64,80},{80,64},{96,112},{112,96},{1... | collective-permute-start | bytes 983048 | tf_op jit(solution)/shard_map/ppermute | solution.py:414
  56.3 1.5 %collective-permute-done.5.refs_3_ = bf16[5,8,32,128]{3,2,1,0:T(8,128)(2,1)S(1)} collective-permute-done((bf16[5,8,32,128]{3,2,1,0:T(8,128)(2,1)S(1)}, bf16[5,8,32,128]{3,2,1,0:T(8,128)(2,1)S(1)}, u32[]{:S(2)}, u32[]{:S(2)}) %collective-permute-start.5) | collective-permute-done | bytes 327712 | tf_op jit(solution)/shard_map/ppermute | solution.py:414
  57.8 5.7 %all-to-all-done.1.got_ref = bf16[16,264,128]{2,1,0:T(8,128)(2,1)S(1)} async-done(((bf16[16,264,128]{2,1,0:T(8,128)(2,1)}), bf16[16,264,128]{2,1,0:T(8,128)(2,1)S(1)}, u32[]{:S(2)}, u32[]{:S(2)}) %all-to-all-start.1) | async-done | bytes 1081376 | tf_op jit(solution)/shard_map/all_to_all | solution.py:432
  63.5 0.0 copy-done
  63.5 1.2 %merge.1 = f32[4,2,8,128]{3,2,1,0:T(8,128)} custom-call(bf16[16,264,128]{2,1,0:T(8,128)(2,1)S(1)} %all-to-all-done.1.got_ref, f32[64,512]{1,0:T(8,128)S(1)} %copy-done, f32[2,128]{1,0:T(2,128)S(1)} %copy-done.1, bf16[4,8,32,128]{3,2,1,0:T(8,128)(2,1)S(1)} %constant_dynamic-update-slice_fusion.refs_0_, ...), custom_call_target="tpu_custom_call" | custom-call | tf_op jit(solution)/shard_map/merge/pallas_call | solution.py:388
  (11 shorter events, 0.1 us)
Async XLA Ops:
  2.0 7.2 %copy-start.3 = (bf16[8,16,128]{2,1,0:T(8,128)(2,1)S(1)}, bf16[8,16,128]{2,1,0:T(8,128)(2,1)}, u32[]{:S(2)}) copy-start(bf16[8,16,128]{2,1,0:T(8,128)(2,1)} %param.9) | copy-start | bytes 98308
  2.0 26.4 %copy-start.2 = (s32[2]{0:T(128)S(1)}, s32[2]{0:T(128)}, u32[]{:S(2)}) copy-start(s32[2]{0:T(128)} %lengths_ref.1) | copy-start | bytes 28
  2.0 26.4 %all-to-all-start = ((bf16[16,72,512]{2,1,0:T(8,128)(2,1)}), bf16[16,72,512]{2,1,0:T(8,128)(2,1)S(1)}, u32[]{:S(2)}, u32[]{:S(2)}) async-start(bf16[16,72,512]{2,1,0:T(8,128)(2,1)} %pack_queries.1), calls=%async_computation | async-start | bytes 2359296 | tf_op jit(solution)/shard_map/all_to_all | solution.py:418
  11.0 13.0 %collective-permute-start = (bf16[1,8,32,128]{3,2,1,0:T(8,128)(2,1)S(1)}, bf16[1,8,32,128]{3,2,1,0:T(8,128)(2,1)S(1)}, u32[]{:S(2)}, u32[]{:S(2)}) collective-permute-start(bf16[1,8,32,128]{3,2,1,0:T(8,128)(2,1)S(1)} %bitcast.2), channel_id=1, source_target_pairs={{128,0},{400,16},{160,32},{432,48},{192,64},{464,80},{224,96},{496... | collective-permute-start | bytes 196616 | tf_op jit(solution)/shard_map/ppermute | solution.py:411
  24.1 12.1 %collective-permute-start.1 = (bf16[2,8,32,128]{3,2,1,0:T(8,128)(2,1)S(1)}, bf16[2,8,32,128]{3,2,1,0:T(8,128)(2,1)S(1)}, u32[]{:S(2)}, u32[]{:S(2)}) collective-permute-start(bf16[2,8,32,128]{3,2,1,0:T(8,128)(2,1)S(1)} %pad_maximum_fusion), channel_id=1, source_target_pairs={{64,0},{464,16},{96,32},{496,48},{128,64},{16,80},{160,96},{48,112... | collective-permute-start | bytes 393224 | tf_op jit(solution)/shard_map/ppermute | solution.py:411
  36.2 27.3 %all-to-all-start.1 = ((bf16[16,264,128]{2,1,0:T(8,128)(2,1)}), bf16[16,264,128]{2,1,0:T(8,128)(2,1)S(1)}, u32[]{:S(2)}, u32[]{:S(2)}) async-start(bf16[16,264,128]{2,1,0:T(8,128)(2,1)} %attend.1), calls=%async_computation.1 | async-start | bytes 2162688 | tf_op jit(solution)/shard_map/all_to_all | solution.py:432
  42.5 21.0 %copy-start = (f32[64,512]{1,0:T(8,128)S(1)}, f32[64,512]{1,0:T(8,128)}, u32[]{:S(2)}) copy-start(f32[64,512]{1,0:T(8,128)} %get-tuple-element.27.fresh_ref) | copy-start | bytes 393220
  42.5 21.0 %copy-start.1 = (f32[2,128]{1,0:T(2,128)S(1)}, f32[2,128]{1,0:T(2,128)}, u32[]{:S(2)}) copy-start(f32[2,128]{1,0:T(2,128)} %get-tuple-element.28.fresh_lse_ref) | copy-start | bytes 3076
  42.6 7.8 %collective-permute-start.2 = (bf16[1,8,32,128]{3,2,1,0:T(8,128)(2,1)S(1)}, bf16[1,8,32,128]{3,2,1,0:T(8,128)(2,1)S(1)}, u32[]{:S(2)}, u32[]{:S(2)}) collective-permute-start(bf16[1,8,32,128]{3,2,1,0:T(8,128)(2,1)S(1)} %slice.3), channel_id=1, source_target_pairs={{464,16},{496,48},{16,80},{48,112},{80,144},{112,176},{144,208},{1... | collective-permute-start | bytes 196616 | tf_op jit(solution)/shard_map/ppermute | solution.py:411
  43.4 10.8 %collective-permute-start.3 = (bf16[4,8,32,128]{3,2,1,0:T(8,128)(2,1)S(1)}, bf16[4,8,32,128]{3,2,1,0:T(8,128)(2,1)S(1)}, u32[]{:S(2)}, u32[]{:S(2)}) collective-permute-start(bf16[4,8,32,128]{3,2,1,0:T(8,128)(2,1)S(1)} %constant_dynamic-update-slice_fusion.refs_0_), channel_id=1, source_target_pairs={{32,0},{496,16},{64,32},{16,48},{96,64},{48,80},{128,96},{80,112},... | collective-permute-start | bytes 786440 | tf_op jit(solution)/shard_map/ppermute | solution.py:411
  50.4 3.9 %collective-permute-start.4 = (bf16[4,8,32,128]{3,2,1,0:T(8,128)(2,1)S(1)}, bf16[4,8,32,128]{3,2,1,0:T(8,128)(2,1)S(1)}, u32[]{:S(2)}, u32[]{:S(2)}) collective-permute-start(bf16[4,8,32,128]{3,2,1,0:T(8,128)(2,1)S(1)} %constant_dynamic-update-slice_fusion.refs_0_), channel_id=1, source_target_pairs={{0,16},{16,0},{32,48},{48,32},{64,80},{80,64},{96,112},{112,96},{1... | collective-permute-start | bytes 786440 | tf_op jit(solution)/shard_map/ppermute | solution.py:414
  54.3 3.5 %collective-permute-start.5 = (bf16[5,8,32,128]{3,2,1,0:T(8,128)(2,1)S(1)}, bf16[5,8,32,128]{3,2,1,0:T(8,128)(2,1)S(1)}, u32[]{:S(2)}, u32[]{:S(2)}) collective-permute-start(bf16[5,8,32,128]{3,2,1,0:T(8,128)(2,1)S(1)} %constant_dynamic-update-slice_fusion.2.refs_1_), channel_id=1, source_target_pairs={{0,16},{16,0},{32,48},{48,32},{64,80},{80,64},{96,112},{112,96},{1... | collective-permute-start | bytes 983048 | tf_op jit(solution)/shard_map/ppermute | solution.py:414

commit v6 on v5

--- a/solution.py
+++ b/solution.py
@@ -259,11 +259,11 @@
     for r in range(rows):
         copies[r][0].wait()
         if r == 0:
+            copies[1][0].start()
             partial_score(0, 0, 256, True)
         copies[r][1].wait()
-        if r + 1 < rows:
-            for copy in copies[r + 1]:
-                copy.start()
+        if r == 0:
+            copies[1][1].start()
         top = None
         for first in range(0, span, CHUNK):
             top = score(r, first, top)
@@ -336,7 +336,9 @@
 
     def place(offset, block):
         chip = (z + own * offset + chips) % chips
-        up[:, pl.ds(pl.multiple_of(chip * depth, depth), depth), :] = block
+        lines = pl.ds(pl.multiple_of(chip * depth, depth), depth)
+        for h in range(heads):
+            up[h // 2, lines, h % 2 * 128 : h % 2 * 128 + 128] = block[h]
 
     for ref, mine, spans in zip(up_refs, (1, 1, -1, -1), offsets):
         for b, offset in enumerate(spans):
@@ -374,9 +376,10 @@
     latent = jnp.concatenate(merged, axis=0).astype(BF16)
     head = lax.broadcasted_iota(jnp.int32, (count, 128), 0) % heads
     result = jnp.zeros((count, 128), F32)
-    for h in range(heads):
-        product = jnp.dot(latent, up[h], preferred_element_type=F32)
-        result = jnp.where(head == h, product, result)
+    for h in range(0, heads, 2):
+        product = jnp.dot(latent, up[h // 2], preferred_element_type=F32)
+        result = jnp.where(head == h, product[:, :128], result)
+        result = jnp.where(head == h + 1, product[:, 128:], result)
     for r in range(rows):
         for s in range(steps):
             first = (r * steps + s) * heads
@@ -390,7 +393,7 @@
         out_shape=jax.ShapeDtypeStruct((steps, rows, heads, width), F32),
         in_specs=[vmem()] * (3 + len(ups)),
         out_specs=vmem(),
-        scratch_shapes=[pltpu.VMEM((heads, LAT, width), BF16)],
+        scratch_shapes=[pltpu.VMEM((heads // 2, LAT, 2 * width), BF16)],
         compiler_params=pltpu.CompilerParams(vmem_limit_bytes=16 * 1024 * 1024),
         name="merge",
     )(got, fresh, fresh_lse, *ups)

time: 65.4 us -> 65.4 us (level)
  the two profiles are of different devices: /device:TPU:64 before, /device:TPU:1 now
where the time goes in v6:
time: 65.4 us; the launch traced here: 64.1 us
  starting transfers between devices  39.8 us (61%)
  Pallas kernels  13.2 us (20%)
  waiting for transfers between devices  6.36 us (10%)
  blocking collectives  4.5 us (7%)
    ppermute x4, starting transfers between devices, from_line(): return lax.ppermute(x, 'dp', pairs)  18.2 us
    pallas_call x1, Pallas kernels, attend(): pl.pallas_call(attend_kernel, out_shape=jax.ShapeDtypeStruct((shards, (st...  7.77 us
    all_to_all x1, starting transfers between devices, body(): gathered = lax.all_to_all(packed, 'ctx', 0, 0, tiled=True)  7.72 us
    all_to_all x1, starting transfers between devices, body(): got = lax.all_to_all(partial, 'ctx', 0, 0, tiled=True)  6.95 us
    ppermute x2, starting transfers between devices, from_core(): return lax.ppermute(x, 'dp', [(i, i ^ 1) for i in range(lines)])  6.9 us
    ppermute x4, waiting for transfers between devices, from_line(): return lax.ppermute(x, 'dp', pairs)  5.09 us
    all_gather x1, blocking collectives, body(): lax.all_gather(value_up, 'dp', axis=1, tiled=True, axis_index_groups=[[2...  4.5 us
    pallas_call x1, Pallas kernels, fresh_part(): pl.pallas_call(fresh_kernel, out_shape=(jax.ShapeDtypeStruct((count, LAT)...  2.08 us
  transfers between devices with their start and end apart: 8, of which 4 were waited for; matrix products, arithmetic and copies ran while one was open for 0% of the time, Pallas kernels for 15%

profile of v6, /device:TPU:1, one launch (start us, length us, event | category | flops | bytes accessed | tf_op | source)
XLA Modules:
  0.0 64.1 jit_solution(389220332665949671)
XLA Ops:
  0.0 2.0 %pack_queries.1 = bf16[16,72,512]{2,1,0:T(8,128)(2,1)} custom-call(bf16[4,2,8,576]{3,2,1,0:T(8,128)(2,1)} %q_ref.3), custom_call_target="tpu_custom_call" | custom-call | tf_op jit(solution)/shard_map/pack_queries/pallas_call | solution.py:57
  2.0 7.7 %all-to-all-start = ((bf16[16,72,512]{2,1,0:T(8,128)(2,1)}), bf16[16,72,512]{2,1,0:T(8,128)(2,1)S(1)}, u32[]{:S(2)}, u32[]{:S(2)}) async-start(bf16[16,72,512]{2,1,0:T(8,128)(2,1)} %pack_queries.1), calls=%async_computation | async-start | bytes 2359296 | tf_op jit(solution)/shard_map/all_to_all | solution.py:421
  9.7 0.0 copy-done.3
  9.7 4.5 %all_gather.3 = bf16[8,32,128]{2,1,0:T(8,128)(2,1)S(1)} all-gather(bf16[8,16,128]{2,1,0:T(8,128)(2,1)S(1)} %copy-done.3), channel_id=1, replica_groups={{0,16},{32,48},{64,80},{96,112},{128,144},{160,176},{192,208},{224,240}..., dimensions={1}, use_global_device_ids=true | all-gather | bytes 98304 | tf_op jit(solution)/shard_map/all_gather | solution.py:423
  14.2 6.8 %collective-permute-start = (bf16[1,8,32,128]{3,2,1,0:T(8,128)(2,1)S(1)}, bf16[1,8,32,128]{3,2,1,0:T(8,128)(2,1)S(1)}, u32[]{:S(2)}, u32[]{:S(2)}) collective-permute-start(bf16[1,8,32,128]{3,2,1,0:T(8,128)(2,1)S(1)} %bitcast.2), channel_id=1, source_target_pairs={{128,0},{400,16},{160,32},{432,48},{192,64},{464,80},{224,96},{496... | collective-permute-start | bytes 196616 | tf_op jit(solution)/shard_map/ppermute | solution.py:414
  21.0 2.1 %fresh_part.1 = (f32[64,512]{1,0:T(8,128)}, f32[2,128]{1,0:T(2,128)}) custom-call(s32[2]{0:T(128)} %lengths_ref.1, bf16[4,2,8,576]{3,2,1,0:T(8,128)(2,1)} %q_ref.3, bf16[4,2,576]{2,1,0:T(2,128)(2,1)} %new_ref.1), custom_call_target="tpu_custom_call" | custom-call | tf_op jit(solution)/shard_map/fresh_part/pallas_call | solution.py:138
  23.1 3.5 %collective-permute-done = bf16[1,8,32,128]{3,2,1,0:T(8,128)(2,1)S(1)} collective-permute-done((bf16[1,8,32,128]{3,2,1,0:T(8,128)(2,1)S(1)}, bf16[1,8,32,128]{3,2,1,0:T(8,128)(2,1)S(1)}, u32[]{:S(2)}, u32[]{:S(2)}) %collective-permute-start) | collective-permute-done | bytes 65568 | tf_op jit(solution)/shard_map/ppermute | solution.py:414
  26.6 4.3 %collective-permute-start.1 = (bf16[2,8,32,128]{3,2,1,0:T(8,128)(2,1)S(1)}, bf16[2,8,32,128]{3,2,1,0:T(8,128)(2,1)S(1)}, u32[]{:S(2)}, u32[]{:S(2)}) collective-permute-start(bf16[2,8,32,128]{3,2,1,0:T(8,128)(2,1)S(1)} %pad_maximum_fusion), channel_id=1, source_target_pairs={{64,0},{464,16},{96,32},{496,48},{128,64},{16,80},{160,96},{48,112... | collective-permute-start | bytes 393224 | tf_op jit(solution)/shard_map/ppermute | solution.py:414
  30.9 0.0 all-to-all-done.q_ref
  30.9 7.8 %attend.1 = bf16[16,264,128]{2,1,0:T(8,128)(2,1)} custom-call(s32[2]{0:T(128)S(1)} %copy-done.2, bf16[16,72,512]{2,1,0:T(8,128)(2,1)S(1)} %all-to-all-done.q_ref, bf16[2,576,1536]{2,1,0:T(8,128)(2,1)} %bitcast.4), custom_call_target="tpu_custom_call" | custom-call | flops 3422552064 | bytes 5898240 | tf_op jit(solution)/shard_map/attend/pallas_call | solution.py:300
  38.7 0.0 collective-permute-done.1
  38.7 6.9 %all-to-all-start.1 = ((bf16[16,264,128]{2,1,0:T(8,128)(2,1)}), bf16[16,264,128]{2,1,0:T(8,128)(2,1)S(1)}, u32[]{:S(2)}, u32[]{:S(2)}) async-start(bf16[16,264,128]{2,1,0:T(8,128)(2,1)} %attend.1), calls=%async_computation.1 | async-start | bytes 2162688 | tf_op jit(solution)/shard_map/all_to_all | solution.py:435
  45.7 0.0 copy-start
  45.7 0.0 copy-start.1
  45.7 3.5 %collective-permute-start.2 = (bf16[1,8,32,128]{3,2,1,0:T(8,128)(2,1)S(1)}, bf16[1,8,32,128]{3,2,1,0:T(8,128)(2,1)S(1)}, u32[]{:S(2)}, u32[]{:S(2)}) collective-permute-start(bf16[1,8,32,128]{3,2,1,0:T(8,128)(2,1)S(1)} %slice.3), channel_id=1, source_target_pairs={{464,16},{496,48},{16,80},{48,112},{80,144},{112,176},{144,208},{1... | collective-permute-start | bytes 196616 | tf_op jit(solution)/shard_map/ppermute | solution.py:414
  49.3 3.7 %collective-permute-start.3 = (bf16[4,8,32,128]{3,2,1,0:T(8,128)(2,1)S(1)}, bf16[4,8,32,128]{3,2,1,0:T(8,128)(2,1)S(1)}, u32[]{:S(2)}, u32[]{:S(2)}) collective-permute-start(bf16[4,8,32,128]{3,2,1,0:T(8,128)(2,1)S(1)} %constant_dynamic-update-slice_fusion.refs_0_), channel_id=1, source_target_pairs={{32,0},{496,16},{64,32},{16,48},{96,64},{48,80},{128,96},{80,112},... | collective-permute-start | bytes 786440 | tf_op jit(solution)/shard_map/ppermute | solution.py:414
  52.9 0.5 collective-permute-done.2
  53.4 3.3 %collective-permute-start.4 = (bf16[4,8,32,128]{3,2,1,0:T(8,128)(2,1)S(1)}, bf16[4,8,32,128]{3,2,1,0:T(8,128)(2,1)S(1)}, u32[]{:S(2)}, u32[]{:S(2)}) collective-permute-start(bf16[4,8,32,128]{3,2,1,0:T(8,128)(2,1)S(1)} %constant_dynamic-update-slice_fusion.refs_0_), channel_id=1, source_target_pairs={{0,16},{16,0},{32,48},{48,32},{64,80},{80,64},{96,112},{112,96},{1... | collective-permute-start | bytes 786440 | tf_op jit(solution)/shard_map/ppermute | solution.py:417
  56.8 1.1 %collective-permute-done.3 = bf16[4,8,32,128]{3,2,1,0:T(8,128)(2,1)S(1)} collective-permute-done((bf16[4,8,32,128]{3,2,1,0:T(8,128)(2,1)S(1)}, bf16[4,8,32,128]{3,2,1,0:T(8,128)(2,1)S(1)}, u32[]{:S(2)}, u32[]{:S(2)}) %collective-permute-start.3) | collective-permute-done | bytes 262176 | tf_op jit(solution)/shard_map/ppermute | solution.py:414
  57.9 0.0 collective-permute-done.4.refs_2_
  57.9 3.6 %collective-permute-start.5 = (bf16[5,8,32,128]{3,2,1,0:T(8,128)(2,1)S(1)}, bf16[5,8,32,128]{3,2,1,0:T(8,128)(2,1)S(1)}, u32[]{:S(2)}, u32[]{:S(2)}) collective-permute-start(bf16[5,8,32,128]{3,2,1,0:T(8,128)(2,1)S(1)} %constant_dynamic-update-slice_fusion.2.refs_1_), channel_id=1, source_target_pairs={{0,16},{16,0},{32,48},{48,32},{64,80},{80,64},{96,112},{112,96},{1... | collective-permute-start | bytes 983048 | tf_op jit(solution)/shard_map/ppermute | solution.py:417
  61.5 1.2 %collective-permute-done.5.refs_3_ = bf16[5,8,32,128]{3,2,1,0:T(8,128)(2,1)S(1)} collective-permute-done((bf16[5,8,32,128]{3,2,1,0:T(8,128)(2,1)S(1)}, bf16[5,8,32,128]{3,2,1,0:T(8,128)(2,1)S(1)}, u32[]{:S(2)}, u32[]{:S(2)}) %collective-permute-start.5) | collective-permute-done | bytes 327712 | tf_op jit(solution)/shard_map/ppermute | solution.py:417
  62.8 0.0 all-to-all-done.1.got_ref
  62.8 1.3 %merge.1 = f32[4,2,8,128]{3,2,1,0:T(8,128)} custom-call(bf16[16,264,128]{2,1,0:T(8,128)(2,1)S(1)} %all-to-all-done.1.got_ref, f32[64,512]{1,0:T(8,128)S(1)} %copy-done, f32[2,128]{1,0:T(2,128)S(1)} %copy-done.1, bf16[4,8,32,128]{3,2,1,0:T(8,128)(2,1)S(1)} %constant_dynamic-update-slice_fusion.refs_0_, ...), custom_call_target="tpu_custom_call" | custom-call | tf_op jit(solution)/shard_map/merge/pallas_call | solution.py:391
  (11 shorter events, 0.1 us)
Async XLA Ops:
  2.0 7.7 %copy-start.3 = (bf16[8,16,128]{2,1,0:T(8,128)(2,1)S(1)}, bf16[8,16,128]{2,1,0:T(8,128)(2,1)}, u32[]{:S(2)}) copy-start(bf16[8,16,128]{2,1,0:T(8,128)(2,1)} %param.9) | copy-start | bytes 98308
  2.0 28.9 %copy-start.2 = (s32[2]{0:T(128)S(1)}, s32[2]{0:T(128)}, u32[]{:S(2)}) copy-start(s32[2]{0:T(128)} %lengths_ref.1) | copy-start | bytes 28
  2.0 28.9 %all-to-all-start = ((bf16[16,72,512]{2,1,0:T(8,128)(2,1)}), bf16[16,72,512]{2,1,0:T(8,128)(2,1)S(1)}, u32[]{:S(2)}, u32[]{:S(2)}) async-start(bf16[16,72,512]{2,1,0:T(8,128)(2,1)} %pack_queries.1), calls=%async_computation | async-start | bytes 2359296 | tf_op jit(solution)/shard_map/all_to_all | solution.py:421
  14.2 12.3 %collective-permute-start = (bf16[1,8,32,128]{3,2,1,0:T(8,128)(2,1)S(1)}, bf16[1,8,32,128]{3,2,1,0:T(8,128)(2,1)S(1)}, u32[]{:S(2)}, u32[]{:S(2)}) collective-permute-start(bf16[1,8,32,128]{3,2,1,0:T(8,128)(2,1)S(1)} %bitcast.2), channel_id=1, source_target_pairs={{128,0},{400,16},{160,32},{432,48},{192,64},{464,80},{224,96},{496... | collective-permute-start | bytes 196616 | tf_op jit(solution)/shard_map/ppermute | solution.py:414
  26.6 12.1 %collective-permute-start.1 = (bf16[2,8,32,128]{3,2,1,0:T(8,128)(2,1)S(1)}, bf16[2,8,32,128]{3,2,1,0:T(8,128)(2,1)S(1)}, u32[]{:S(2)}, u32[]{:S(2)}) collective-permute-start(bf16[2,8,32,128]{3,2,1,0:T(8,128)(2,1)S(1)} %pad_maximum_fusion), channel_id=1, source_target_pairs={{64,0},{464,16},{96,32},{496,48},{128,64},{16,80},{160,96},{48,112... | collective-permute-start | bytes 393224 | tf_op jit(solution)/shard_map/ppermute | solution.py:414
  38.7 24.0 %all-to-all-start.1 = ((bf16[16,264,128]{2,1,0:T(8,128)(2,1)}), bf16[16,264,128]{2,1,0:T(8,128)(2,1)S(1)}, u32[]{:S(2)}, u32[]{:S(2)}) async-start(bf16[16,264,128]{2,1,0:T(8,128)(2,1)} %attend.1), calls=%async_computation.1 | async-start | bytes 2162688 | tf_op jit(solution)/shard_map/all_to_all | solution.py:435
  45.7 17.1 %copy-start = (f32[64,512]{1,0:T(8,128)S(1)}, f32[64,512]{1,0:T(8,128)}, u32[]{:S(2)}) copy-start(f32[64,512]{1,0:T(8,128)} %get-tuple-element.27.fresh_ref) | copy-start | bytes 393220
  45.7 17.1 %copy-start.1 = (f32[2,128]{1,0:T(2,128)S(1)}, f32[2,128]{1,0:T(2,128)}, u32[]{:S(2)}) copy-start(f32[2,128]{1,0:T(2,128)} %get-tuple-element.28.fresh_lse_ref) | copy-start | bytes 3076
  45.7 7.7 %collective-permute-start.2 = (bf16[1,8,32,128]{3,2,1,0:T(8,128)(2,1)S(1)}, bf16[1,8,32,128]{3,2,1,0:T(8,128)(2,1)S(1)}, u32[]{:S(2)}, u32[]{:S(2)}) collective-permute-start(bf16[1,8,32,128]{3,2,1,0:T(8,128)(2,1)S(1)} %slice.3), channel_id=1, source_target_pairs={{464,16},{496,48},{16,80},{48,112},{80,144},{112,176},{144,208},{1... | collective-permute-start | bytes 196616 | tf_op jit(solution)/shard_map/ppermute | solution.py:414
  49.3 8.6 %collective-permute-start.3 = (bf16[4,8,32,128]{3,2,1,0:T(8,128)(2,1)S(1)}, bf16[4,8,32,128]{3,2,1,0:T(8,128)(2,1)S(1)}, u32[]{:S(2)}, u32[]{:S(2)}) collective-permute-start(bf16[4,8,32,128]{3,2,1,0:T(8,128)(2,1)S(1)} %constant_dynamic-update-slice_fusion.refs_0_), channel_id=1, source_target_pairs={{32,0},{496,16},{64,32},{16,48},{96,64},{48,80},{128,96},{80,112},... | collective-permute-start | bytes 786440 | tf_op jit(solution)/shard_map/ppermute | solution.py:414
  53.4 4.5 %collective-permute-start.4 = (bf16[4,8,32,128]{3,2,1,0:T(8,128)(2,1)S(1)}, bf16[4,8,32,128]{3,2,1,0:T(8,128)(2,1)S(1)}, u32[]{:S(2)}, u32[]{:S(2)}) collective-permute-start(bf16[4,8,32,128]{3,2,1,0:T(8,128)(2,1)S(1)} %constant_dynamic-update-slice_fusion.refs_0_), channel_id=1, source_target_pairs={{0,16},{16,0},{32,48},{48,32},{64,80},{80,64},{96,112},{112,96},{1... | collective-permute-start | bytes 786440 | tf_op jit(solution)/shard_map/ppermute | solution.py:417
  57.9 4.8 %collective-permute-start.5 = (bf16[5,8,32,128]{3,2,1,0:T(8,128)(2,1)S(1)}, bf16[5,8,32,128]{3,2,1,0:T(8,128)(2,1)S(1)}, u32[]{:S(2)}, u32[]{:S(2)}) collective-permute-start(bf16[5,8,32,128]{3,2,1,0:T(8,128)(2,1)S(1)} %constant_dynamic-update-slice_fusion.2.refs_1_), channel_id=1, source_target_pairs={{0,16},{16,0},{32,48},{48,32},{64,80},{80,64},{96,112},{112,96},{1... | collective-permute-start | bytes 983048 | tf_op jit(solution)/shard_map/ppermute | solution.py:417
